TPU v7x, 256 devices: a whole 4x4x8 slice. The times are simulated.
256 devices in a mesh: sec: 64 (over z, x_hi, y), row: 4 (over x_lo, core).
Axes of the slice: x: 4 (x_hi: 2, x_lo: 2; x = x_hi * 2 + x_lo), y: 4, z: 8, core: 2. Of those that a mesh axis runs over, the one named last changes fastest.
Arguments:
- image: bfloat16 [256, 512, 640], P('sec', 'row'), may hold values from -8 to 8, as said below
- grid_shift: int32 [256, 4, 5, 2], P('sec', 'row'), may hold values from -32 to 32
- partner_step: int32 [256, 2], P('sec'), may hold values from 1 to 2
- tissue: int32 [256, 4, 5], P('sec', 'row'), may hold values 0 or 1
Outputs:
- correlation: float32 [256, 2, 4, 5, 16384], P('sec', None, 'row')
Inputs may be any that keep to these rules, and one draw needn't show every extreme that they name: `image`: each section is a drifting, possibly rescaled copy of one common pattern plus independent speckle.
All inputs are finite; a program needn't handle non-finite values. No bound on the sum of `tissue` on one device may be relied on, other than what follows from the above.
Results may differ from a plain program's by a relative error of at most 0.012.
Values may be sent and summed in bfloat16 or wider, within the bound.
A program may use at most 128 MiB of HBM per device.

v0:
```python
import math

import jax
import jax.numpy as jnp
from jax import lax
from jax.sharding import PartitionSpec as P

PC = 5
PATCH = 256
REACH = 32
SHIFTS = 128


def extended(cells, sides, width):
    for axis, dim in sides:
        count = lax.axis_size(axis)
        ends = count - 1
        head = lax.slice_in_dim(cells, 0, width, axis=dim)
        tail = lax.slice_in_dim(cells, cells.shape[dim] - width, cells.shape[dim], axis=dim)
        cells = jnp.concatenate(
            [
                lax.ppermute(tail, axis, [(i, (i + 1) % count) for i in range(ends)]),
                cells,
                lax.ppermute(head, axis, [((i + 1) % count, i) for i in range(ends)]),
            ],
            axis=dim,
        )
    return cells


def shifted(shard, axis, by):
    devices = lax.axis_size(axis)
    pairs = [(i, i + by) for i in range(devices) if 0 <= i + by < devices]
    return lax.ppermute(shard, axis, pairs)


def forward_tables():
    indices = jnp.arange(PATCH, dtype=jnp.int32)
    product = indices[:, None] * indices[None, :] % PATCH
    phases = product.astype(jnp.float32) * (2.0 * math.pi / PATCH)
    return (jnp.cos(phases).astype(jnp.bfloat16), jnp.sin(phases).astype(jnp.bfloat16))


def inverse_tables():
    indices = jnp.arange(PATCH, dtype=jnp.int32)
    displace = jnp.arange(SHIFTS, dtype=jnp.int32) - SHIFTS // 2
    product = displace[:, None] * indices[None, :] % PATCH
    phases = product.astype(jnp.float32) * (2.0 * math.pi / PATCH)
    return (jnp.cos(phases).astype(jnp.bfloat16), jnp.sin(phases).astype(jnp.bfloat16))


def normalize(patches):
    values = patches.astype(jnp.float32)
    centre = jnp.mean(values, axis=(1, 2), keepdims=True)
    deviate = values - centre
    spread = jnp.mean(deviate * deviate, axis=(1, 2), keepdims=True)
    return (deviate * lax.rsqrt(spread + 1e-05)).astype(jnp.bfloat16)


def transform(patches, cosine, sine):
    right_re = jnp.einsum(
        "bij,jk->bik", patches, cosine, preferred_element_type=jnp.float32
    ).astype(jnp.bfloat16)
    right_im = (
        -jnp.einsum("bij,jk->bik", patches, sine, preferred_element_type=jnp.float32)
    ).astype(jnp.bfloat16)
    spec_re = jnp.einsum(
        "ij,bjk->bik", cosine, right_re, preferred_element_type=jnp.float32
    ) + jnp.einsum("ij,bjk->bik", sine, right_im, preferred_element_type=jnp.float32)
    spec_im = jnp.einsum(
        "ij,bjk->bik", cosine, right_im, preferred_element_type=jnp.float32
    ) - jnp.einsum("ij,bjk->bik", sine, right_re, preferred_element_type=jnp.float32)
    return (spec_re.astype(jnp.bfloat16), spec_im.astype(jnp.bfloat16))


def correlate(own_re, own_im, part_re, part_im, back_re, back_im):
    real_a = own_re.astype(jnp.float32)
    imag_a = own_im.astype(jnp.float32)
    real_b = part_re.astype(jnp.float32)
    imag_b = part_im.astype(jnp.float32)
    cross_re = (real_a * real_b + imag_a * imag_b).astype(jnp.bfloat16)
    cross_im = (real_a * imag_b - imag_a * real_b).astype(jnp.bfloat16)
    half_re = jnp.einsum(
        "uk,bkl->bul", back_re, cross_re, preferred_element_type=jnp.float32
    ) - jnp.einsum("uk,bkl->bul", back_im, cross_im, preferred_element_type=jnp.float32)
    half_im = jnp.einsum(
        "uk,bkl->bul", back_re, cross_im, preferred_element_type=jnp.float32
    ) + jnp.einsum("uk,bkl->bul", back_im, cross_re, preferred_element_type=jnp.float32)
    half_re = half_re.astype(jnp.bfloat16)
    half_im = half_im.astype(jnp.bfloat16)
    maps = jnp.einsum(
        "bul,vl->buv", half_re, back_re, preferred_element_type=jnp.float32
    ) - jnp.einsum("bul,vl->buv", half_im, back_im, preferred_element_type=jnp.float32)
    maps = maps / float(PATCH * PATCH)
    return maps.reshape(maps.shape[0], SHIFTS * SHIFTS)


def add_margin(strips):
    return extended(strips, (("row", 1),), PATCH // 4 + REACH)


def plain_spectra(windows, cosine, sine):
    margin = PATCH // 4 + REACH
    half = PATCH // 2

    def plain_one(plane):
        wide = jnp.pad(plane, ((0, 0), (margin, margin)))
        strip = wide[:, REACH : REACH + half * (PC + 1)].reshape(PATCH, PC + 1, half)
        joined = jnp.concatenate([strip[:, :-1], strip[:, 1:]], axis=2)
        return transform(normalize(jnp.transpose(joined, (1, 0, 2))), cosine, sine)

    return lax.map(plain_one, windows)


def on_device(image, grid_shift, partner_step, tissue):
    sec_count = image.shape[0]
    margin = PATCH // 4 + REACH
    half = PATCH // 2
    cosine, sine = forward_tables()
    back_re, back_im = inverse_tables()
    padded = add_margin(image)
    windows = padded[:, REACH : REACH + PATCH]
    leading = shifted(windows[:2], "sec", -1)
    plain_re, plain_im = plain_spectra(jnp.concatenate([windows, leading], 0), cosine, sine)
    padcols = jnp.pad(padded, ((0, 0), (0, 0), (margin, margin)))
    pcol_ids = jnp.arange(PC, dtype=jnp.int32)

    def section_maps(items):
        plane, shifts, steps, weight, near_re, near_im, far_re, far_im = items
        starts_row = REACH + shifts[0, :, 0]
        starts_col = half * pcol_ids + REACH + shifts[0, :, 1]

        def cut_one(first_row, first_col):
            return lax.dynamic_slice(plane, (first_row, first_col), (PATCH, PATCH))

        own_re, own_im = transform(
            normalize(jax.vmap(cut_one)(starts_row, starts_col)), cosine, sine
        )
        scale = weight.astype(jnp.float32)
        slots = []
        for slot in range(2):
            chosen = steps[slot] == 1
            part_re = jnp.where(chosen, near_re, far_re)
            part_im = jnp.where(chosen, near_im, far_im)
            maps = correlate(own_re, own_im, part_re, part_im, back_re, back_im).reshape(
                1, PC, SHIFTS * SHIFTS
            )
            slots.append(maps * scale[:, :, None])
        return jnp.stack(slots, 0)

    items = (
        padcols,
        grid_shift,
        partner_step,
        tissue,
        plain_re[1 : sec_count + 1],
        plain_im[1 : sec_count + 1],
        plain_re[2 : sec_count + 2],
        plain_im[2 : sec_count + 2],
    )
    return lax.map(section_maps, items)


def solution(mesh):
    return jax.shard_map(
        on_device,
        mesh=mesh,
        in_specs=(
            P("sec", "row", None),
            P("sec", "row", None, None),
            P("sec", None),
            P("sec", "row", None),
        ),
        out_specs=P("sec", None, "row", None, None),
        check_vma=False,
    )
```

profile of v0, /device:TPU:193, one launch (start us, length us, event | category | flops | bytes accessed | tf_op | source)
XLA Modules:
  0.0 257.1 jit_solution(822599047255113403)
XLA Ops:
  1.3 3.7 %collective-permute-start = (bf16[4,96,640]{2,1,0:T(8,128)(2,1)S(1)}, bf16[4,96,640]{2,1,0:T(8,128)(2,1)S(1)}, u32[]{:S(2)}, u32[]{:S(2)}) collective-permute-start(bf16[4,96,640]{2,1,0:T(8,128)(2,1)S(1)} %get-tuple-element.546), channel_id=1, source_target_pairs={{0,1},{1,2},{2,3},{4,5},{5,6},{6,7},{8,9},{9,10},{10,11},{12,13},{... | collective-permute-start | bytes 1474568 | tf_op jit(solution)/shard_map/ppermute | solution.py:22
  7.0 3.8 %collective-permute-done = bf16[4,96,640]{2,1,0:T(8,128)(2,1)S(1)} collective-permute-done((bf16[4,96,640]{2,1,0:T(8,128)(2,1)S(1)}, bf16[4,96,640]{2,1,0:T(8,128)(2,1)S(1)}, u32[]{:S(2)}, u32[]{:S(2)}) %collective-permute-start) | collective-permute-done | bytes 491552 | tf_op jit(solution)/shard_map/ppermute | solution.py:22
  10.9 4.6 %collective-permute-done.1 = bf16[4,96,640]{2,1,0:T(8,128)(2,1)S(1)} collective-permute-done((bf16[4,96,640]{2,1,0:T(8,128)(2,1)S(1)}, bf16[4,96,640]{2,1,0:T(8,128)(2,1)S(1)}, u32[]{:S(2)}, u32[]{:S(2)}) %collective-permute-start.1) | collective-permute-done | bytes 491552 | tf_op jit(solution)/shard_map/ppermute | solution.py:24
  15.7 6.9 %collective-permute-start.2 = (bf16[2,256,640]{2,1,0:T(8,128)(2,1)S(1)}, bf16[2,256,640]{2,1,0:T(8,128)(2,1)}, u32[]{:S(2)}, u32[]{:S(2)}) collective-permute-start(bf16[2,256,640]{2,1,0:T(8,128)(2,1)S(1)} %slice.109), channel_id=1, source_target_pairs={{4,0},{8,4},{12,8},{16,12},{20,16},{24,20},{28,24},{32,28},{36,32}... | collective-permute-start | bytes 1966088 | tf_op jit(solution)/shard_map/ppermute | solution.py:34
  22.7 2.4 pad.11
  25.1 6.0 %collective-permute-done.2 = bf16[2,256,640]{2,1,0:T(8,128)(2,1)} collective-permute-done((bf16[2,256,640]{2,1,0:T(8,128)(2,1)S(1)}, bf16[2,256,640]{2,1,0:T(8,128)(2,1)}, u32[]{:S(2)}, u32[]{:S(2)}) %collective-permute-start.2) | collective-permute-done | bytes 655392 | tf_op jit(solution)/shard_map/ppermute | solution.py:34
  31.2 2.6 %pad_maximum_fusion.1 = bf16[6,256,640]{2,1,0:T(8,128)(2,1)} fusion(bf16[2,256,640]{2,1,0:T(8,128)(2,1)} %collective-permute-done.2, bf16[4,256,640]{2,1,0:T(8,128)(2,1)S(1)} %slice.108), kind=kLoop, calls=%fused_computation.233 | loop fusion | flops 983040 | bytes 3932160 | tf_op jit(solution)/shard_map/concatenate | solution.py:124
  33.8 69.4 %while.36 = (s32[]{:T(128)}, bf16[6,5,256,256]{2,3,1,0:T(8,128)(2,1)}, bf16[6,5,256,256]{2,3,1,0:T(8,128)(2,1)}, bf16[6,256,640]{2,1,0:T(8,128)(2,1)}, s32[]{:T(128)}) while((s32[]{:T(128)}, bf16[6,5,256,256]{2,3,1,0:T(8,128)(2,1)}, bf16[6,5,256,256]{2,3,1,0:T(8,128)(2,1)}, bf16[6,256,640]{2,1,0:T(8,128)(2,1)}, ...), condition=%wide.region_3.4_spmd.clone.clone, body=%wide.region_0.3_spmd.clone.clone.sunk | while | flops 1023344640 | bytes 16450845 | solution.py:112
  62.9 2.2 fusion.327
  66.4 2.2 fusion.325
  103.2 7.6 %fusion.222 = (bf16[4,5,256,256]{2,3,1,0:T(8,128)(2,1)}, bf16[4,5,256,256]{2,3,1,0:T(8,128)(2,1)}, bf16[4,5,256,256]{2,3,1,0:T(8,128)(2,1)}, bf16[4,5,256,256]{2,3,1,0:T(8,128)(2,1)}) fusion(bf16[6,5,256,256]{2,3,1,0:T(8,128)(2,1)} %get-tuple-element.323, bf16[6,5,256,256]{2,3,1,0:T(8,128)(2,1)} %get-tuple-element.322), kind=kLoop, calls=%fused_computation.241 | loop fusion | bytes 20971520 | tf_op jit(solution)/shard_map/slice | solution.py:159
  110.8 146.3 %while.38 = (s32[]{:T(128)}, f32[4,2,1,5,16384]{4,2,3,1,0:T(1,128)}, bf16[4,320,832]{2,1,0:T(8,128)(2,1)S(1)}, s32[4,1,5,2]{2,3,1,0:T(2,128)}, s32[4,2]{0,1:T(2,...) while((s32[]{:T(128)}, ...), condition=%wide.region_7.8_spmd.clone.clone.clone, body=%wide.region_4.7_spmd.clone.clone.clone.sunk | while | flops 1874657280 | bytes 55727536 | solution.py:161
  111.8 10.3 %while.39 = (s32[]{:T(128)}, bf16[320,832]{1,0:T(8,128)(2,1)S(1)}, s32[5,2]{0,1:T(2,128)S(1)}, bf16[5,256,256]{2,1,0:T(8,128)(2,1)S(1)}, s32[]{:T(128)}) while((s32[]{:T(128)}, bf16[320,832]{1,0:T(8,128)(2,1)S(1)}, s32[5,2]{0,1:T(2,128)S(1)}, bf16[5,256,256]{2,1,0:T(8,128)(2,1)S(1)}, s32[]{:T(128)}) %tuple.106), condition=%wide.while_cond, body=%wide.while_body.sunk | while | flops 2 | bytes 262253 | solution.py:134
  131.1 3.7 %fusion.366 = (bf16[5,256,256]{1,2,0:T(8,128)(2,1)S(1)}, bf16[5,256,256]{1,2,0:T(8,128)(2,1)S(1)}, bf16[5,256,256]{1,2,0:T(8,128)(2,1)S(1)}, bf16[5,256,256]{1,2,0:T(8,128)(2,1)S(1)}) fusion(f32[5,256,256]{1,2,0:T(8,128)S(1)} %fusion.363, bf16[4,5,256,256]{2,3,1,0:T(8,128)(2,1)} %get-tuple-element.771, s32[]{:T(128)} %get-tuple-element.750, ...), kind=kOutput, calls=%fused_computation.99.clone.1 | convolution fusion | flops 177602560 | bytes 8519686 | tf_op jit(solution)/shard_map/while/body/eval_jaxpr/ij,bjk->bik/dot_general | solution.py:69
  138.4 2.3 fusion.375
  148.3 10.3 %while.39 = (s32[]{:T(128)}, bf16[320,832]{1,0:T(8,128)(2,1)S(1)}, s32[5,2]{0,1:T(2,128)S(1)}, bf16[5,256,256]{2,1,0:T(8,128)(2,1)S(1)}, s32[]{:T(128)}) while((s32[]{:T(128)}, bf16[320,832]{1,0:T(8,128)(2,1)S(1)}, s32[5,2]{0,1:T(2,128)S(1)}, bf16[5,256,256]{2,1,0:T(8,128)(2,1)S(1)}, s32[]{:T(128)}) %tuple.106), condition=%wide.while_cond, body=%wide.while_body.sunk | while | flops 2 | bytes 262253 | solution.py:134
  167.6 3.7 %fusion.366 = (bf16[5,256,256]{1,2,0:T(8,128)(2,1)S(1)}, bf16[5,256,256]{1,2,0:T(8,128)(2,1)S(1)}, bf16[5,256,256]{1,2,0:T(8,128)(2,1)S(1)}, bf16[5,256,256]{1,2,0:T(8,128)(2,1)S(1)}) fusion(f32[5,256,256]{1,2,0:T(8,128)S(1)} %fusion.363, bf16[4,5,256,256]{2,3,1,0:T(8,128)(2,1)} %get-tuple-element.771, s32[]{:T(128)} %get-tuple-element.750, ...), kind=kOutput, calls=%fused_computation.99.clone.1 | convolution fusion | flops 177602560 | bytes 8519686 | tf_op jit(solution)/shard_map/while/body/eval_jaxpr/ij,bjk->bik/dot_general | solution.py:69
  174.9 2.3 fusion.375
  184.8 10.3 %while.39 = (s32[]{:T(128)}, bf16[320,832]{1,0:T(8,128)(2,1)S(1)}, s32[5,2]{0,1:T(2,128)S(1)}, bf16[5,256,256]{2,1,0:T(8,128)(2,1)S(1)}, s32[]{:T(128)}) while((s32[]{:T(128)}, bf16[320,832]{1,0:T(8,128)(2,1)S(1)}, s32[5,2]{0,1:T(2,128)S(1)}, bf16[5,256,256]{2,1,0:T(8,128)(2,1)S(1)}, s32[]{:T(128)}) %tuple.106), condition=%wide.while_cond, body=%wide.while_body.sunk | while | flops 2 | bytes 262253 | solution.py:134
  204.1 3.7 %fusion.366 = (bf16[5,256,256]{1,2,0:T(8,128)(2,1)S(1)}, bf16[5,256,256]{1,2,0:T(8,128)(2,1)S(1)}, bf16[5,256,256]{1,2,0:T(8,128)(2,1)S(1)}, bf16[5,256,256]{1,2,0:T(8,128)(2,1)S(1)}) fusion(f32[5,256,256]{1,2,0:T(8,128)S(1)} %fusion.363, bf16[4,5,256,256]{2,3,1,0:T(8,128)(2,1)} %get-tuple-element.771, s32[]{:T(128)} %get-tuple-element.750, ...), kind=kOutput, calls=%fused_computation.99.clone.1 | convolution fusion | flops 177602560 | bytes 8519686 | tf_op jit(solution)/shard_map/while/body/eval_jaxpr/ij,bjk->bik/dot_general | solution.py:69
  211.4 2.3 fusion.375
  221.4 10.3 %while.39 = (s32[]{:T(128)}, bf16[320,832]{1,0:T(8,128)(2,1)S(1)}, s32[5,2]{0,1:T(2,128)S(1)}, bf16[5,256,256]{2,1,0:T(8,128)(2,1)S(1)}, s32[]{:T(128)}) while((s32[]{:T(128)}, bf16[320,832]{1,0:T(8,128)(2,1)S(1)}, s32[5,2]{0,1:T(2,128)S(1)}, bf16[5,256,256]{2,1,0:T(8,128)(2,1)S(1)}, s32[]{:T(128)}) %tuple.106), condition=%wide.while_cond, body=%wide.while_body.sunk | while | flops 2 | bytes 262253 | solution.py:134
  240.7 3.7 %fusion.366 = (bf16[5,256,256]{1,2,0:T(8,128)(2,1)S(1)}, bf16[5,256,256]{1,2,0:T(8,128)(2,1)S(1)}, bf16[5,256,256]{1,2,0:T(8,128)(2,1)S(1)}, bf16[5,256,256]{1,2,0:T(8,128)(2,1)S(1)}) fusion(f32[5,256,256]{1,2,0:T(8,128)S(1)} %fusion.363, bf16[4,5,256,256]{2,3,1,0:T(8,128)(2,1)} %get-tuple-element.771, s32[]{:T(128)} %get-tuple-element.750, ...), kind=kOutput, calls=%fused_computation.99.clone.1 | convolution fusion | flops 177602560 | bytes 8519686 | tf_op jit(solution)/shard_map/while/body/eval_jaxpr/ij,bjk->bik/dot_general | solution.py:69
  247.9 2.3 fusion.375
  (291 shorter events, 184.3 us)
Async XLA Ops:
  0.0 10.8 %copy-start.3 = (bf16[4,128,640]{2,1,0:T(8,128)(2,1)S(1)}, bf16[4,128,640]{2,1,0:T(8,128)(2,1)}, u32[]{:S(2)}) copy-start(bf16[4,128,640]{2,1,0:T(8,128)(2,1)} %param.8) | copy-start | bytes 1966084
  1.3 9.4 %collective-permute-start = (bf16[4,96,640]{2,1,0:T(8,128)(2,1)S(1)}, bf16[4,96,640]{2,1,0:T(8,128)(2,1)S(1)}, u32[]{:S(2)}, u32[]{:S(2)}) collective-permute-start(bf16[4,96,640]{2,1,0:T(8,128)(2,1)S(1)} %get-tuple-element.546), channel_id=1, source_target_pairs={{0,1},{1,2},{2,3},{4,5},{5,6},{6,7},{8,9},{9,10},{10,11},{12,13},{... | collective-permute-start | bytes 1474568 | tf_op jit(solution)/shard_map/ppermute | solution.py:22
  5.0 10.5 %collective-permute-start.1 = (bf16[4,96,640]{2,1,0:T(8,128)(2,1)S(1)}, bf16[4,96,640]{2,1,0:T(8,128)(2,1)S(1)}, u32[]{:S(2)}, u32[]{:S(2)}) collective-permute-start(bf16[4,96,640]{2,1,0:T(8,128)(2,1)S(1)} %get-tuple-element.545), channel_id=1, source_target_pairs={{1,0},{2,1},{3,2},{5,4},{6,5},{7,6},{9,8},{10,9},{11,10},{13,12},{... | collective-permute-start | bytes 1474568 | tf_op jit(solution)/shard_map/ppermute | solution.py:24
  15.6 7.0 %copy-start.2 = (bf16[4,320,640]{2,1,0:T(8,128)(2,1)}, bf16[4,320,640]{2,1,0:T(8,128)(2,1)S(1)}, u32[]{:S(2)}) copy-start(bf16[4,320,640]{2,1,0:T(8,128)(2,1)S(1)} %constant_dynamic-update-slice_fusion) | copy-start | bytes 4915204
  15.7 15.5 %collective-permute-start.2 = (bf16[2,256,640]{2,1,0:T(8,128)(2,1)S(1)}, bf16[2,256,640]{2,1,0:T(8,128)(2,1)}, u32[]{:S(2)}, u32[]{:S(2)}) collective-permute-start(bf16[2,256,640]{2,1,0:T(8,128)(2,1)S(1)} %slice.109), channel_id=1, source_target_pairs={{4,0},{8,4},{12,8},{16,12},{20,16},{24,20},{28,24},{32,28},{36,32}... | collective-permute-start | bytes 1966088 | tf_op jit(solution)/shard_map/ppermute | solution.py:34
  103.2 7.6 %copy-start.4 = (s32[4,2]{0,1:T(2,128)S(1)}, s32[4,2]{0,1:T(2,128)}, u32[]{:S(2)}) copy-start(s32[4,2]{0,1:T(2,128)} %param.10) | copy-start | bytes 100
  111.0 14.3 %copy-start = (bf16[4,320,832]{2,1,0:T(8,128)(2,1)}, bf16[4,320,832]{2,1,0:T(8,128)(2,1)S(1)}, u32[]{:S(2)}) copy-start(bf16[4,320,832]{2,1,0:T(8,128)(2,1)S(1)} %get-tuple-element.767) | copy-start | bytes 6389764 | tf_op jit(solution)/shard_map/while
  145.9 1.6 copy-start.1
  147.6 14.3 %copy-start = (bf16[4,320,832]{2,1,0:T(8,128)(2,1)}, bf16[4,320,832]{2,1,0:T(8,128)(2,1)S(1)}, u32[]{:S(2)}) copy-start(bf16[4,320,832]{2,1,0:T(8,128)(2,1)S(1)} %get-tuple-element.767) | copy-start | bytes 6389764 | tf_op jit(solution)/shard_map/while
  182.4 1.6 copy-start.1
  184.1 14.3 %copy-start = (bf16[4,320,832]{2,1,0:T(8,128)(2,1)}, bf16[4,320,832]{2,1,0:T(8,128)(2,1)S(1)}, u32[]{:S(2)}) copy-start(bf16[4,320,832]{2,1,0:T(8,128)(2,1)S(1)} %get-tuple-element.767) | copy-start | bytes 6389764 | tf_op jit(solution)/shard_map/while
  218.9 1.6 copy-start.1
  220.6 14.3 %copy-start = (bf16[4,320,832]{2,1,0:T(8,128)(2,1)}, bf16[4,320,832]{2,1,0:T(8,128)(2,1)S(1)}, u32[]{:S(2)}) copy-start(bf16[4,320,832]{2,1,0:T(8,128)(2,1)S(1)} %get-tuple-element.767) | copy-start | bytes 6389764 | tf_op jit(solution)/shard_map/while
  255.4 1.6 copy-start.1
where the time goes:
time: 261 us; the launch traced here: 257 us
  matrix products  139 us (53%)
  local copies, waits for them, and re-layouts  72.2 us (28%)
  waiting for transfers between devices  14.5 us (6%)
  starting transfers between devices  12.5 us (5%)
  other arithmetic  12.2 us (5%)
  loops' own time  6.72 us (3%)
    gather x60, local copies, waits for them, and re-layouts  40.6 us
    dot_general x10, matrix products, transform(): jnp.einsum('ij,bjk->bik', sine, right_im, preferred_element_type=jnp.floa...  27.5 us
    dot_general x10, matrix products, transform(): jnp.einsum('ij,bjk->bik', sine, right_re, preferred_element_type=jnp.floa...  17.9 us
    dot_general x8, matrix products, correlate(): jnp.einsum('bul,vl->buv', half_im, back_im, preferred_element_type=jnp.fl...  14.5 us
    dot_general x10, matrix products, transform(): jnp.einsum('bij,jk->bik', patches, sine, preferred_element_type=jnp.float32)  13.9 us
    dot_general x10, matrix products, transform(): jnp.einsum('bij,jk->bik', patches, cosine, preferred_element_type=jnp.flo...  13.7 us
    dot_general x8, matrix products, correlate(): jnp.einsum('bul,vl->buv', half_re, back_re, preferred_element_type=jnp.fl...  13.4 us
    dot_general x10, matrix products, transform(): jnp.einsum('ij,bjk->bik', cosine, right_re, preferred_element_type=jnp.fl...  12.7 us
  transfers between devices with their start and end apart: 3, of which 3 were waited for; matrix products, arithmetic and copies ran while one was open for 1% of the time, Pallas kernels for 0%

commit v1 on v0

v1 whole, which is shorter than its diff:
```python
import functools

import jax
import jax.numpy as jnp
import ml_dtypes
import numpy as np
from jax import lax
from jax.experimental import pallas as pl
from jax.experimental.pallas import tpu as pltpu
from jax.sharding import PartitionSpec as P

PC = 5
PATCH = 256
HALF = 128
REACH = 32
HALO = 96
SHIFTS = 128
WIDE = 4 * HALF


def angle(product):
    return 2.0 * np.pi * (product % PATCH) / PATCH


def row_table():
    k = np.arange(HALF)[:, None]
    r = np.arange(PATCH)[None, :]
    sine = np.sin(angle(k * r))
    sine[0] = 1.0 - 2.0 * (np.arange(PATCH) % 2)
    return np.concatenate([np.cos(angle(k * r)), sine], 0).astype(ml_dtypes.bfloat16)


def col_tables():
    c = np.arange(HALF)[:, None]
    out = []
    for odd in (0, 1):
        ell = 2 * np.arange(HALF)[None, :] + odd
        cos, sin = np.cos(angle(ell * c)), np.sin(angle(ell * c))
        out.append(np.block([[cos, -sin], [-sin, -cos]]))
    return np.stack(out).astype(ml_dtypes.bfloat16)


def back_col_tables():
    v = np.arange(SHIFTS)[None, :] - SHIFTS // 2
    out = []
    for odd in (0, 1):
        ell = 2 * np.arange(HALF)[:, None] + odd
        cos, sin = np.cos(angle(ell * v)), np.sin(angle(ell * v))
        out.append(np.block([[cos, sin], [-sin, cos]]))
    return np.stack(out).astype(ml_dtypes.bfloat16)


def back_row_tables():
    rows = SHIFTS + 2 * REACH
    u = np.arange(rows + 16)[:, None] - (SHIFTS // 2 + REACH)
    k = np.arange(HALF)[None, :]
    weight = np.where(k == 0, 1.0, 2.0)
    sine = -weight * np.sin(angle(u * k))
    sine[:, 0] = 1.0 - 2.0 * (u[:, 0] % 2)
    full = np.concatenate([weight * np.cos(angle(u * k)), sine], 1)
    return np.stack([full[q : q + rows] for q in range(16)]).astype(ml_dtypes.bfloat16)


def phase_table():
    s = np.arange(2 * REACH + 1)[:, None] - REACH
    even = 2 * np.arange(HALF)[None, :]
    parts = [f(angle(ell * s)) for f in (np.cos, np.sin) for ell in (even, even + 1)]
    return np.concatenate(parts, 1).astype(np.float32)[:, None, :]


def dot(a, b):
    return jnp.dot(a, b, preferred_element_type=jnp.float32)


def folded(own, above, below, tile, start):
    lanes = slice(tile * HALF, (tile + 1) * HALF)
    low = above[0:64, lanes]
    high = below[32:96, lanes]
    rows = lax.broadcasted_iota(jnp.int32, (64, HALF), 0) + 32
    mixed = jnp.where(rows >= start, low.astype(jnp.float32), high.astype(jnp.float32)).astype(jnp.bfloat16)
    return jnp.concatenate([below[0:32, lanes], mixed, above[64:96, lanes], own[:, lanes]], 0)


def window(own, above, below, c, row_start, col_start):
    right = folded(own, above, below, c, row_start)
    zero = jnp.zeros((PATCH, HALF), jnp.bfloat16)
    far = folded(own, above, below, c - 1, row_start) if c > 0 else zero
    near = folded(own, above, below, c + 1, row_start) if c < PC - 1 else zero
    lanes = lax.broadcasted_iota(jnp.int32, (PATCH, HALF), 1)
    left = jnp.where(lanes >= col_start, far.astype(jnp.float32), near.astype(jnp.float32)).astype(jnp.bfloat16)
    return jnp.concatenate([left, right], 1)


def forward(own, above, below, starts, phases, tab_row, tab_col, nyq, spec, spec_nyq, rstd):
    first = lax.broadcasted_iota(jnp.int32, (8, HALF), 0) == 0

    def top(block):
        return block[0:8], block[8:]

    for c in range(PC):
        x = window(own, above, below, c, *starts[c])
        part = dot(tab_row[...], x)
        lo, hi = part[:, :HALF], part[:, HALF:]
        even, odd = lo + hi, lo - hi
        ce, se, co, so = even[:HALF], even[HALF:], odd[:HALF], odd[HALF:]
        head, tail = top(ce)
        centre = jnp.mean(head[0:1], axis=1, keepdims=True)
        head = jnp.where(first, head - centre, head)
        ce = jnp.concatenate([head, tail], 0)
        square = jnp.zeros((8, HALF), jnp.float32)
        edge = jnp.zeros((8, HALF), jnp.float32)
        for block in (ce, se, co, so):
            sq = block * block
            square = square + jnp.sum(sq.reshape(HALF // 8, 8, HALF), axis=0)
            edge = edge + sq[0:8]
        total = 2.0 * square - jnp.where(first, edge, 0.0)
        var = jnp.sum(jnp.sum(total, axis=0, keepdims=True), axis=1, keepdims=True) * (
            HALF / float(PATCH**4)
        )
        rstd[c] = jnp.broadcast_to(lax.rsqrt(var + 1e-05), (8, HALF))
        he, te = top(se)
        ho, to = top(so)
        nyq[c : c + 1, :HALF] = he[0:1]
        nyq[c : c + 1, HALF:] = ho[0:1]
        se = jnp.concatenate([jnp.where(first, 0.0, he), te], 0)
        so = jnp.concatenate([jnp.where(first, 0.0, ho), to], 0)
        fe = dot(jnp.concatenate([ce, se], 1).astype(jnp.bfloat16), tab_col[0])
        fo = dot(jnp.concatenate([co, so], 1).astype(jnp.bfloat16), tab_col[1])
        f = [fe[:, :HALF], fe[:, HALF:], fo[:, :HALF], fo[:, HALF:]]
        if phases is not None:
            f = turned(f, phases[c])
        spec[c] = jnp.concatenate(f, 1).astype(jnp.bfloat16)
    zero = jnp.zeros((16, HALF), jnp.bfloat16)
    ne = jnp.concatenate([nyq[:, :HALF].astype(jnp.bfloat16), zero], 1)
    no = jnp.concatenate([nyq[:, HALF:].astype(jnp.bfloat16), zero], 1)
    fe, fo = dot(ne, tab_col[0]), dot(no, tab_col[1])
    f = [fe[:, :HALF], fe[:, HALF:], fo[:, :HALF], fo[:, HALF:]]
    if phases is not None:
        rows = [jnp.concatenate([p[c] for c in range(PC)] + [jnp.zeros((16 - PC, HALF), jnp.float32)], 0) for p in zip(*[split4(q) for q in phases])]
        f = turned(f, rows)
    spec_nyq[...] = jnp.concatenate(f, 1).astype(jnp.bfloat16)


def split4(p):
    return [p[:, i * HALF : (i + 1) * HALF] for i in range(4)]


def turned(f, phase):
    ce, co, se, so = phase if isinstance(phase, list) else split4(phase)
    return [
        f[0] * ce - f[1] * se,
        f[0] * se + f[1] * ce,
        f[2] * co - f[3] * so,
        f[2] * so + f[3] * co,
    ]


def crossed(a, b):
    out = []
    for base in (0, 2 * HALF):
        re, im = slice(base, base + HALF), slice(base + HALF, base + 2 * HALF)
        are, aim = a[:, re].astype(jnp.float32), a[:, im].astype(jnp.float32)
        bre, bim = b[:, re].astype(jnp.float32), b[:, im].astype(jnp.float32)
        g = jnp.concatenate([are * bre + aim * bim, are * bim - aim * bre], 1)
        out.append(g.astype(jnp.bfloat16))
    return out


def kernel(
    shift_ref, step_ref, tissue_ref, img, above, below, nxt, nxt_above, nxt_below,
    tab_row, tab_col, tab_bcol, tab_brow, tab_phase, out,
    nyq, own_spec, own_nyq, own_rstd, spec, spec_nyq, rstd,
):
    secs = img.shape[0]
    nyq[...] = jnp.zeros_like(nyq)

    def plain(rows, up, down, slot):
        forward(rows, up, down, [(64, 64)] * PC, None, tab_row, tab_col, nyq, spec.at[slot], spec_nyq.at[slot], rstd.at[slot])

    def pairs(s):
        for c in range(PC):
            stage = []
            scales = []
            for slot in range(2):
                part = s + step_ref[s, slot] - 1
                ge, go = crossed(own_spec[c], spec[part, c])
                xe, xo = crossed(own_nyq[...], spec_nyq[part])
                ge = jnp.concatenate([ge, xe], 0)
                go = jnp.concatenate([go, xo], 0)
                g = dot(ge, tab_bcol[0]) + dot(go, tab_bcol[1])
                stage.append(g)
                scales.append(own_rstd[c] * rstd[part, c] * (tissue_ref[s, 0, c].astype(jnp.float32) / float(PATCH * PATCH)))
            first = lax.broadcasted_iota(jnp.int32, (8, HALF), 0) == 0
            cols = []
            for g in stage:
                edge = jnp.broadcast_to(g[HALF + c : HALF + c + 1, :HALF], (8, HALF))
                im = g[:HALF, HALF:]
                head = jnp.where(first, edge, im[0:8])
                cols.append(jnp.concatenate([g[:HALF, :HALF], head, im[8:]], 0))
            right = jnp.concatenate(cols, 1).astype(jnp.bfloat16)
            at = REACH - shift_ref[s, 0, c, 0]
            fine = lax.rem(at, 16)
            start = pl.multiple_of(at - fine, 16)
            left = tab_brow[fine, pl.ds(start, SHIFTS), :]
            maps = dot(left, right)
            for slot in range(2):
                piece = maps[:, slot * HALF : (slot + 1) * HALF].reshape(SHIFTS // 8, 8, HALF)
                out[s, slot, c] = (piece * scales[slot][None]).reshape(SHIFTS, SHIFTS)

    def own(s):
        starts = [(shift_ref[s, 0, c, 0] + 64, shift_ref[s, 0, c, 1] + 64) for c in range(PC)]
        phases = [tab_phase[shift_ref[s, 0, c, 1] + REACH] for c in range(PC)]
        forward(img.at[s], above.at[s], below.at[s], starts, phases, tab_row, tab_col, nyq, own_spec, own_nyq, own_rstd)

    for j in range(2):
        plain(nxt.at[j], nxt_above.at[j], nxt_below.at[j], secs - 1 + j)

    def local(i, carry):
        plain(img.at[i + 1], above.at[i + 1], below.at[i + 1], i)
        return carry

    lax.fori_loop(0, secs - 1, local, 0)

    def each(s, carry):
        own(s)
        pairs(s)
        return carry

    lax.fori_loop(0, secs, each, 0)


def from_row(block, by):
    count = lax.axis_size("row")
    return lax.ppermute(block, "row", [(i - by, i) for i in range(count) if 0 <= i - by < count])


def from_next(block, by):
    secs, rows = lax.axis_size("sec"), lax.axis_size("row")
    pairs = [
        ((s + 1) * rows + r - by, s * rows + r)
        for s in range(secs - 1)
        for r in range(rows)
        if 0 <= r - by < rows
    ]
    return lax.ppermute(block, ("sec", "row"), pairs)


def compute(image, above, below, nxt, nxt_above, nxt_below, grid_shift, partner_step, tissue):
    secs = image.shape[0]
    tables = [row_table(), col_tables(), back_col_tables(), back_row_tables(), phase_table()]
    smem = pl.BlockSpec(memory_space=pltpu.SMEM)
    vmem = pl.BlockSpec(memory_space=pltpu.VMEM)
    return pl.pallas_call(
        kernel,
        out_shape=jax.ShapeDtypeStruct((secs, 2, PC, SHIFTS, SHIFTS), jnp.float32),
        in_specs=[smem] * 3 + [vmem] * 11,
        out_specs=vmem,
        scratch_shapes=[
            pltpu.VMEM((16, PATCH), jnp.float32),
            pltpu.VMEM((PC, HALF, WIDE), jnp.bfloat16),
            pltpu.VMEM((16, WIDE), jnp.bfloat16),
            pltpu.VMEM((PC, 8, HALF), jnp.float32),
            pltpu.VMEM((secs + 1, PC, HALF, WIDE), jnp.bfloat16),
            pltpu.VMEM((secs + 1, 16, WIDE), jnp.bfloat16),
            pltpu.VMEM((secs + 1, PC, 8, HALF), jnp.float32),
        ],
        compiler_params=pltpu.CompilerParams(vmem_limit_bytes=56 * 1024 * 1024),
        cost_estimate=pl.CostEstimate(flops=6_000_000_000, bytes_accessed=8_000_000, transcendentals=0),
    )(
        grid_shift, partner_step, tissue, image, above, below, nxt, nxt_above, nxt_below,
        *[jnp.asarray(t) for t in tables],
    )


def on_device(image, grid_shift, partner_step, tissue):
    above = from_row(image[:, HALF - HALO :], 1)
    below = from_row(image[:, :HALO], -1)
    nxt = from_next(image[:2], 0)
    nxt_above = from_next(image[:2, HALF - HALO :], 1)
    nxt_below = from_next(image[:2, :HALO], -1)
    maps = compute(image, above, below, nxt, nxt_above, nxt_below, grid_shift, partner_step, tissue)
    return maps.reshape(image.shape[0], 2, 1, PC, SHIFTS * SHIFTS)


def solution(mesh):
    return jax.shard_map(
        on_device,
        mesh=mesh,
        in_specs=(
            P("sec", "row", None),
            P("sec", "row", None, None),
            P("sec", None),
            P("sec", "row", None),
        ),
        out_specs=P("sec", None, "row", None, None),
        check_vma=False,
    )
```

time: 261 us -> 52.4 us (0.20)
  the two profiles are of different devices: /device:TPU:193 before, /device:TPU:126 now
where the time goes in v1:
time: 52.4 us; the launch traced here: 52.1 us
  waiting for transfers between devices  19.5 us (37%)
  Pallas kernels  15.3 us (29%)
  starting transfers between devices  11.9 us (23%)
  local copies, waits for them, and re-layouts  5.35 us (10%)
    ppermute x3, waiting for transfers between devices, from_next(): return lax.ppermute(block, ('sec', 'row'), pairs)  19.5 us
    pallas_call x1, Pallas kernels, compute(): pl.pallas_call(kernel, out_shape=jax.ShapeDtypeStruct((secs, 2, PC, SHIFT...  15.3 us
    ppermute x3, starting transfers between devices, from_next(): return lax.ppermute(block, ('sec', 'row'), pairs)  7.57 us
    ppermute x2, starting transfers between devices, from_row(): lax.ppermute(block, 'row', [(i - by, i) for i in range(count) if 0 <= i -...  4.35 us
    unnamed x16, local copies, waits for them, and re-layouts  2.97 us
    slice x1, local copies, waits for them, and re-layouts, on_device(): below = from_row(image[:, :HALO], -1)  1.33 us
  transfers between devices with their start and end apart: 5, of which 2 were waited for; matrix products, arithmetic and copies ran while one was open for 5% of the time, Pallas kernels for 0%

profile of v1, /device:TPU:126, one launch (start us, length us, event | category | flops | bytes accessed | tf_op | source)
XLA Modules:
  0.0 52.1 jit_solution(10514497426763335685)
XLA Ops:
  0.0 0.0 copy-start
  0.0 1.3 %fusion.1 = (bf16[4,96,640]{2,1,0:T(8,128)(2,1)S(1)}, bf16[4,96,640]{2,1,0:T(8,128)(2,1)S(1)}) fusion(bf16[4,128,640]{2,1,0:T(8,128)(2,1)} %img.1), kind=kLoop, calls=%fused_computation.1 | loop fusion | bytes 1966080 | tf_op jit(solution)/shard_map/slice | solution.py:277
  1.3 2.2 %collective-permute-start.1 = (bf16[4,96,640]{2,1,0:T(8,128)(2,1)S(1)}, bf16[4,96,640]{2,1,0:T(8,128)(2,1)S(1)}, u32[]{:S(2)}, u32[]{:S(2)}) collective-permute-start(bf16[4,96,640]{2,1,0:T(8,128)(2,1)S(1)} %get-tuple-element.7), channel_id=1, source_target_pairs={{1,0},{2,1},{3,2},{5,4},{6,5},{7,6},{9,8},{10,9},{11,10},{13,12},{... | collective-permute-start | bytes 1474568 | tf_op jit(solution)/shard_map/ppermute | solution.py:234
  3.5 2.2 %collective-permute-start = (bf16[4,96,640]{2,1,0:T(8,128)(2,1)S(1)}, bf16[4,96,640]{2,1,0:T(8,128)(2,1)S(1)}, u32[]{:S(2)}, u32[]{:S(2)}) collective-permute-start(bf16[4,96,640]{2,1,0:T(8,128)(2,1)S(1)} %get-tuple-element.8), channel_id=1, source_target_pairs={{0,1},{1,2},{2,3},{4,5},{5,6},{6,7},{8,9},{9,10},{10,11},{12,13},{... | collective-permute-start | bytes 1474568 | tf_op jit(solution)/shard_map/ppermute | solution.py:234
  5.7 1.0 %slice.17 = bf16[2,128,640]{2,1,0:T(8,128)(2,1)S(1)} slice(bf16[4,128,640]{2,1,0:T(8,128)(2,1)} %img.1), slice={[0:2], [0:128], [0:640]} | slice | bytes 655360 | tf_op jit(solution)/shard_map/slice | solution.py:278
  6.7 2.7 %collective-permute-start.2 = (bf16[2,128,640]{2,1,0:T(8,128)(2,1)S(1)}, bf16[2,128,640]{2,1,0:T(8,128)(2,1)}, u32[]{:S(2)}, u32[]{:S(2)}) collective-permute-start(bf16[2,128,640]{2,1,0:T(8,128)(2,1)S(1)} %slice.17), channel_id=1, source_target_pairs={{4,0},{5,1},{6,2},{7,3},{8,4},{9,5},{10,6},{11,7},{12,8},{13,9},{1... | collective-permute-start | bytes 983048 | tf_op jit(solution)/shard_map/ppermute | solution.py:245
  9.4 0.0 copy-done
  9.4 3.0 %collective-permute-start.4 = (bf16[2,96,640]{2,1,0:T(8,128)(2,1)S(1)}, bf16[2,96,640]{2,1,0:T(8,128)(2,1)S(1)}, u32[]{:S(2)}, u32[]{:S(2)}) collective-permute-start(bf16[2,96,640]{2,1,0:T(8,128)(2,1)S(1)} %get-tuple-element.5), channel_id=1, source_target_pairs={{5,0},{6,1},{7,2},{9,4},{10,5},{11,6},{13,8},{14,9},{15,10},{17,12... | collective-permute-start | bytes 737288 | tf_op jit(solution)/shard_map/ppermute | solution.py:245
  12.4 1.9 %collective-permute-start.3 = (bf16[2,96,640]{2,1,0:T(8,128)(2,1)S(1)}, bf16[2,96,640]{2,1,0:T(8,128)(2,1)S(1)}, u32[]{:S(2)}, u32[]{:S(2)}) collective-permute-start(bf16[2,96,640]{2,1,0:T(8,128)(2,1)S(1)} %get-tuple-element.6), channel_id=1, source_target_pairs={{4,1},{5,2},{6,3},{8,5},{9,6},{10,7},{12,9},{13,10},{14,11},{16,13... | collective-permute-start | bytes 737288 | tf_op jit(solution)/shard_map/ppermute | solution.py:245
  14.4 0.0 copy-done.2
  14.4 0.7 %copy.14.step_ref = s32[4,2]{1,0:T(4,128)} copy(s32[4,2]{0,1:T(2,128)S(1)} %copy-done.2) | data formatting | bytes 64 | tf_op args[2]
  15.0 0.0 copy-done.1
  15.1 0.7 %copy.13.shift_ref = s32[4,1,5,2]{3,2,1,0:T(8,128)} copy(s32[4,1,5,2]{2,3,1,0:T(2,128)S(1)} %copy-done.1) | data formatting | bytes 320 | tf_op args[1]
  15.8 11.2 %collective-permute-done.4.nxt_below = bf16[2,96,640]{2,1,0:T(8,128)(2,1)S(1)} collective-permute-done((bf16[2,96,640]{2,1,0:T(8,128)(2,1)S(1)}, bf16[2,96,640]{2,1,0:T(8,128)(2,1)S(1)}, u32[]{:S(2)}, u32[]{:S(2)}) %collective-permute-start.4) | collective-permute-done | bytes 245792 | tf_op jit(solution)/shard_map/ppermute | solution.py:245
  27.0 8.3 %collective-permute-done.3.nxt_above = bf16[2,96,640]{2,1,0:T(8,128)(2,1)S(1)} collective-permute-done((bf16[2,96,640]{2,1,0:T(8,128)(2,1)S(1)}, bf16[2,96,640]{2,1,0:T(8,128)(2,1)S(1)}, u32[]{:S(2)}, u32[]{:S(2)}) %collective-permute-start.3) | collective-permute-done | bytes 245792 | tf_op jit(solution)/shard_map/ppermute | solution.py:245
  35.2 0.0 collective-permute-done.2.nxt
  35.2 0.0 collective-permute-done.1.below
  35.3 0.0 copy-start.3
  35.3 0.0 collective-permute-done.above
  35.3 0.0 copy-done.5
  35.3 0.7 %copy-done.6 = bf16[2,96,640]{2,1,0:T(8,128)(2,1)} copy-done((bf16[2,96,640]{2,1,0:T(8,128)(2,1)}, bf16[2,96,640]{2,1,0:T(8,128)(2,1)S(1)}, u32[]{:S(2)}) %copy-start.6) | copy-done | bytes 245784
  35.9 0.2 copy-done.3
  36.1 0.8 %copy-done.4 = bf16[4,96,640]{2,1,0:T(8,128)(2,1)} copy-done((bf16[4,96,640]{2,1,0:T(8,128)(2,1)}, bf16[4,96,640]{2,1,0:T(8,128)(2,1)S(1)}, u32[]{:S(2)}) %copy-start.4) | copy-done | bytes 491544
  36.9 15.3 %shard_map.91 = f32[4,2,5,128,128]{4,3,2,1,0:T(8,128)} custom-call(s32[4,1,5,2]{3,2,1,0:T(8,128)} %copy.13.shift_ref, s32[4,2]{1,0:T(4,128)} %copy.14.step_ref, s32[4,1,5]{2,1,0:T(1,128)} %tissue_ref.1, bf16[4,128,640]{2,1,0:T(8,128)(2,1)} %img.1, bf16[4,96,640]{2,1,0:T(8,128)(2,1)} %copy-done.4, bf16[4,96,640]{2,1,0:T(8,128)(2,1)} %copy-done.3, ...), custom_call_target="tpu_custom_call" | custom-call | flops 6000000000 | bytes 8000000 | tf_op jit(solution)/shard_map/pallas_call | solution.py:253
  (6 shorter events, 0.0 us)
Async XLA Ops:
  0.0 9.4 %copy-start = (bf16[4,128,640]{2,1,0:T(8,128)(2,1)S(1)}, bf16[4,128,640]{2,1,0:T(8,128)(2,1)}, u32[]{:S(2)}) copy-start(bf16[4,128,640]{2,1,0:T(8,128)(2,1)} %img.1) | copy-start | bytes 1966084
  0.0 14.4 %copy-start.2 = (s32[4,2]{0,1:T(2,128)S(1)}, s32[4,2]{0,1:T(2,128)}, u32[]{:S(2)}) copy-start(s32[4,2]{0,1:T(2,128)} %param.11) | copy-start | bytes 100
  0.0 15.0 %copy-start.1 = (s32[4,1,5,2]{2,3,1,0:T(2,128)S(1)}, s32[4,1,5,2]{2,3,1,0:T(2,128)}, u32[]{:S(2)}) copy-start(s32[4,1,5,2]{2,3,1,0:T(2,128)} %param.10) | copy-start | bytes 484
  1.3 33.9 %collective-permute-start.1 = (bf16[4,96,640]{2,1,0:T(8,128)(2,1)S(1)}, bf16[4,96,640]{2,1,0:T(8,128)(2,1)S(1)}, u32[]{:S(2)}, u32[]{:S(2)}) collective-permute-start(bf16[4,96,640]{2,1,0:T(8,128)(2,1)S(1)} %get-tuple-element.7), channel_id=1, source_target_pairs={{1,0},{2,1},{3,2},{5,4},{6,5},{7,6},{9,8},{10,9},{11,10},{13,12},{... | collective-permute-start | bytes 1474568 | tf_op jit(solution)/shard_map/ppermute | solution.py:234
  3.5 31.7 %collective-permute-start = (bf16[4,96,640]{2,1,0:T(8,128)(2,1)S(1)}, bf16[4,96,640]{2,1,0:T(8,128)(2,1)S(1)}, u32[]{:S(2)}, u32[]{:S(2)}) collective-permute-start(bf16[4,96,640]{2,1,0:T(8,128)(2,1)S(1)} %get-tuple-element.8), channel_id=1, source_target_pairs={{0,1},{1,2},{2,3},{4,5},{5,6},{6,7},{8,9},{9,10},{10,11},{12,13},{... | collective-permute-start | bytes 1474568 | tf_op jit(solution)/shard_map/ppermute | solution.py:234
  6.7 28.5 %collective-permute-start.2 = (bf16[2,128,640]{2,1,0:T(8,128)(2,1)S(1)}, bf16[2,128,640]{2,1,0:T(8,128)(2,1)}, u32[]{:S(2)}, u32[]{:S(2)}) collective-permute-start(bf16[2,128,640]{2,1,0:T(8,128)(2,1)S(1)} %slice.17), channel_id=1, source_target_pairs={{4,0},{5,1},{6,2},{7,3},{8,4},{9,5},{10,6},{11,7},{12,8},{13,9},{1... | collective-permute-start | bytes 983048 | tf_op jit(solution)/shard_map/ppermute | solution.py:245
  9.4 17.5 %collective-permute-start.4 = (bf16[2,96,640]{2,1,0:T(8,128)(2,1)S(1)}, bf16[2,96,640]{2,1,0:T(8,128)(2,1)S(1)}, u32[]{:S(2)}, u32[]{:S(2)}) collective-permute-start(bf16[2,96,640]{2,1,0:T(8,128)(2,1)S(1)} %get-tuple-element.5), channel_id=1, source_target_pairs={{5,0},{6,1},{7,2},{9,4},{10,5},{11,6},{13,8},{14,9},{15,10},{17,12... | collective-permute-start | bytes 737288 | tf_op jit(solution)/shard_map/ppermute | solution.py:245
  12.4 22.8 %collective-permute-start.3 = (bf16[2,96,640]{2,1,0:T(8,128)(2,1)S(1)}, bf16[2,96,640]{2,1,0:T(8,128)(2,1)S(1)}, u32[]{:S(2)}, u32[]{:S(2)}) collective-permute-start(bf16[2,96,640]{2,1,0:T(8,128)(2,1)S(1)} %get-tuple-element.6), channel_id=1, source_target_pairs={{4,1},{5,2},{6,3},{8,5},{9,6},{10,7},{12,9},{13,10},{14,11},{16,13... | collective-permute-start | bytes 737288 | tf_op jit(solution)/shard_map/ppermute | solution.py:245
  26.9 8.3 %copy-start.5 = (bf16[2,96,640]{2,1,0:T(8,128)(2,1)}, bf16[2,96,640]{2,1,0:T(8,128)(2,1)S(1)}, u32[]{:S(2)}) copy-start(bf16[2,96,640]{2,1,0:T(8,128)(2,1)S(1)} %collective-permute-done.4.nxt_below) | copy-start | bytes 737284
  35.2 0.7 %copy-start.6 = (bf16[2,96,640]{2,1,0:T(8,128)(2,1)}, bf16[2,96,640]{2,1,0:T(8,128)(2,1)S(1)}, u32[]{:S(2)}) copy-start(bf16[2,96,640]{2,1,0:T(8,128)(2,1)S(1)} %collective-permute-done.3.nxt_above) | copy-start | bytes 737284
  35.3 0.8 %copy-start.3 = (bf16[4,96,640]{2,1,0:T(8,128)(2,1)}, bf16[4,96,640]{2,1,0:T(8,128)(2,1)S(1)}, u32[]{:S(2)}) copy-start(bf16[4,96,640]{2,1,0:T(8,128)(2,1)S(1)} %collective-permute-done.1.below) | copy-start | bytes 1474564
  36.1 0.8 %copy-start.4 = (bf16[4,96,640]{2,1,0:T(8,128)(2,1)}, bf16[4,96,640]{2,1,0:T(8,128)(2,1)S(1)}, u32[]{:S(2)}) copy-start(bf16[4,96,640]{2,1,0:T(8,128)(2,1)S(1)} %collective-permute-done.above) | copy-start | bytes 1474564

commit v2 on v1

--- a/solution.py
+++ b/solution.py
@@ -50,22 +50,33 @@
     return np.stack(out).astype(ml_dtypes.bfloat16)
 
 
-def back_row_tables():
-    rows = SHIFTS + 2 * REACH
-    u = np.arange(rows + 16)[:, None] - (SHIFTS // 2 + REACH)
+def back_row_table():
+    u = np.arange(SHIFTS)[:, None] - SHIFTS // 2
     k = np.arange(HALF)[None, :]
     weight = np.where(k == 0, 1.0, 2.0)
     sine = -weight * np.sin(angle(u * k))
     sine[:, 0] = 1.0 - 2.0 * (u[:, 0] % 2)
-    full = np.concatenate([weight * np.cos(angle(u * k)), sine], 1)
-    return np.stack([full[q : q + rows] for q in range(16)]).astype(ml_dtypes.bfloat16)
-
-
-def phase_table():
+    return np.concatenate([weight * np.cos(angle(u * k)), sine], 1).astype(np.float32)
+
+
+def phase_table(frequencies):
     s = np.arange(2 * REACH + 1)[:, None] - REACH
-    even = 2 * np.arange(HALF)[None, :]
-    parts = [f(angle(ell * s)) for f in (np.cos, np.sin) for ell in (even, even + 1)]
-    return np.concatenate(parts, 1).astype(np.float32)[:, None, :]
+    parts = np.concatenate([f(angle(ell[None, :] * s)) for f, ell in frequencies], 1)
+    high = parts.astype(ml_dtypes.bfloat16)
+    low = (parts - high.astype(np.float64)).astype(ml_dtypes.bfloat16)
+    out = np.zeros((PATCH, parts.shape[1]), ml_dtypes.bfloat16)
+    out[: len(s)], out[HALF : HALF + len(s)] = high, low
+    return out
+
+
+def col_phases():
+    even = 2 * np.arange(HALF)
+    return phase_table([(f, ell) for f in (np.cos, np.sin) for ell in (even, even + 1)])
+
+
+def row_phases():
+    k = np.arange(HALF)
+    return phase_table([(np.cos, k), (np.cos, np.where(k == 0, HALF, k)), (np.sin, k)])
 
 
 def dot(a, b):
@@ -74,6 +85,8 @@
 
 def folded(own, above, below, tile, start):
     lanes = slice(tile * HALF, (tile + 1) * HALF)
+    if start is None:
+        return jnp.concatenate([below[0:64, lanes], above[32:96, lanes], own[:, lanes]], 0)
     low = above[0:64, lanes]
     high = below[32:96, lanes]
     rows = lax.broadcasted_iota(jnp.int32, (64, HALF), 0) + 32
@@ -166,125 +179,279 @@
     return out
 
 
+def remote(src, dst, send, recv, where):
+    return pltpu.make_async_remote_copy(
+        src_ref=src, dst_ref=dst, send_sem=send, recv_sem=recv, device_id=where, device_id_type=pl.DeviceIdType.MESH
+    )
+
+
 def kernel(
-    shift_ref, step_ref, tissue_ref, img, above, below, nxt, nxt_above, nxt_below,
-    tab_row, tab_col, tab_bcol, tab_brow, tab_phase, out,
-    nyq, own_spec, own_nyq, own_rstd, spec, spec_nyq, rstd,
+    secs_axis, rows_axis,
+    shift_ref, step_ref, tissue_ref, img, *refs,
 ):
-    secs = img.shape[0]
+    tables, refs = refs[:6], refs[6:]
+    out, refs = refs[0], refs[1:]
+    tabs, refs = refs[:6], refs[6:]
+    (strip, above, below, pcol, prow, nyq, own_spec, own_nyq, own_rstd, spec, spec_nyq, rstd, stage,
+     tab_sem, img_sem, out_sem, up_send, up_recv, down_send, down_recv, sec_send, sec_recv) = refs
+    tab_row, tab_col, tab_bcol, tab_brow, tab_pcol, tab_prow = tabs
+    secs = own_spec.shape[0]
+    sec, row = lax.axis_index("sec"), lax.axis_index("row")
+    has_up, has_down = row > 0, row < rows_axis - 1
+    has_prev, has_next = sec > 0, sec < secs_axis - 1
+    up, down, prev, following = (sec, row - 1), (sec, row + 1), (sec - 1, row), (sec + 1, row)
+    sides = ((has_up, up), (has_down, down), (has_prev, prev), (has_next, following))
+
+    barrier = pltpu.get_barrier_semaphore()
+    for there, where in sides:
+        @pl.when(there)
+        def _():
+            pl.semaphore_signal(barrier, inc=1, device_id=where, device_id_type=pl.DeviceIdType.MESH)
+
+    img_copy = pltpu.make_async_copy(img, strip.at[0:secs], img_sem)
+    img_copy.start()
+    loads = [pltpu.make_async_copy(t, v, tab_sem.at[i]) for i, (t, v) in enumerate(zip(tables, tabs))]
+    for load in loads:
+        load.start()
+
+    pl.semaphore_wait(barrier, sum(there.astype(jnp.int32) for there, _ in sides))
+
+    def to_prev(j):
+        return remote(img.at[j], strip.at[secs + j], sec_send.at[j], sec_recv.at[j], prev)
+
+    def to_down(t):
+        return remote(img.at[t, HALF - HALO : HALF], above.at[t], down_send.at[t], down_recv.at[t], down)
+
+    def to_up(t):
+        return remote(img.at[t, 0:HALO], below.at[t], up_send.at[t], up_recv.at[t], up)
+
+    def relay_down(j):
+        t = secs + j
+        return remote(strip.at[t, HALF // 2 : HALF], above.at[t, HALO - HALF // 2 : HALO], down_send.at[t], down_recv.at[t], down)
+
+    def relay_up(j):
+        t = secs + j
+        return remote(strip.at[t, 0 : HALF // 2], below.at[t, 0 : HALF // 2], up_send.at[t], up_recv.at[t], up)
+
+    @pl.when(has_prev)
+    def _():
+        for j in range(2):
+            to_prev(j).start()
+
+    @pl.when(has_down)
+    def _():
+        for t in range(secs):
+            to_down(t).start()
+
+    @pl.when(has_up)
+    def _():
+        for t in range(secs):
+            to_up(t).start()
+
+    @pl.when(jnp.logical_not(has_up))
+    def _():
+        above[...] = jnp.zeros_like(above)
+
+    @pl.when(jnp.logical_not(has_down))
+    def _():
+        below[...] = jnp.zeros_like(below)
+
+    @pl.when(jnp.logical_not(has_next))
+    def _():
+        strip[secs:] = jnp.zeros((2, HALF, strip.shape[2]), jnp.bfloat16)
+        above[secs:] = jnp.zeros((2, HALO, strip.shape[2]), jnp.bfloat16)
+        below[secs:] = jnp.zeros((2, HALO, strip.shape[2]), jnp.bfloat16)
+
     nyq[...] = jnp.zeros_like(nyq)
-
-    def plain(rows, up, down, slot):
-        forward(rows, up, down, [(64, 64)] * PC, None, tab_row, tab_col, nyq, spec.at[slot], spec_nyq.at[slot], rstd.at[slot])
+    img_copy.wait()
+    for load in loads:
+        load.wait()
+
+    rows = lax.broadcasted_iota(jnp.int32, (8 * secs, PATCH), 0)
+    lanes = lax.broadcasted_iota(jnp.int32, (8 * secs, PATCH), 1)
+    for axis, table, phase in ((0, tab_prow, prow), (1, tab_pcol, pcol)):
+        wanted = jnp.zeros_like(lanes)
+        for s in range(secs):
+            for c in range(PC):
+                wanted = jnp.where(rows == 8 * s + c, shift_ref[s, 0, axis, c] + REACH, wanted)
+        chosen = jnp.logical_or(lanes == wanted, lanes == wanted + HALF)
+        picked = dot(chosen.astype(jnp.float32).astype(jnp.bfloat16), table[...])
+        phase[...] = picked.reshape(secs, 8, picked.shape[1])
+
+    def plain(t):
+        forward(
+            strip.at[t], above.at[t], below.at[t], [(None, 64)] * PC, None, tab_row, tab_col, nyq,
+            spec.at[t - 1], spec_nyq.at[t - 1], rstd.at[t - 1],
+        )
+
+    def own(s):
+        starts = [(shift_ref[s, 0, 0, c] + 64, shift_ref[s, 0, 1, c] + 64) for c in range(PC)]
+        phases = [pcol[s, c : c + 1] for c in range(PC)]
+        forward(
+            strip.at[s], above.at[s], below.at[s], starts, phases, tab_row, tab_col, nyq,
+            own_spec.at[s], own_nyq.at[s], own_rstd.at[s],
+        )
+
+    first = lax.broadcasted_iota(jnp.int32, (8, HALF), 0) == 0
 
     def pairs(s):
         for c in range(PC):
-            stage = []
-            scales = []
-            for slot in range(2):
-                part = s + step_ref[s, slot] - 1
-                ge, go = crossed(own_spec[c], spec[part, c])
-                xe, xo = crossed(own_nyq[...], spec_nyq[part])
+            cols = []
+            for part in (s, s + 1):
+                ge, go = crossed(own_spec[s, c], spec[part, c])
+                xe, xo = crossed(own_nyq[s], spec_nyq[part])
                 ge = jnp.concatenate([ge, xe], 0)
                 go = jnp.concatenate([go, xo], 0)
                 g = dot(ge, tab_bcol[0]) + dot(go, tab_bcol[1])
-                stage.append(g)
-                scales.append(own_rstd[c] * rstd[part, c] * (tissue_ref[s, 0, c].astype(jnp.float32) / float(PATCH * PATCH)))
-            first = lax.broadcasted_iota(jnp.int32, (8, HALF), 0) == 0
-            cols = []
-            for g in stage:
                 edge = jnp.broadcast_to(g[HALF + c : HALF + c + 1, :HALF], (8, HALF))
                 im = g[:HALF, HALF:]
                 head = jnp.where(first, edge, im[0:8])
                 cols.append(jnp.concatenate([g[:HALF, :HALF], head, im[8:]], 0))
             right = jnp.concatenate(cols, 1).astype(jnp.bfloat16)
-            at = REACH - shift_ref[s, 0, c, 0]
-            fine = lax.rem(at, 16)
-            start = pl.multiple_of(at - fine, 16)
-            left = tab_brow[fine, pl.ds(start, SHIFTS), :]
+            turn = prow[s, c : c + 1]
+            cos, cos_edge, sin = turn[:, :HALF], turn[:, HALF : 2 * HALF], turn[:, 2 * HALF :]
+            bc, bs = tab_brow[:, :HALF], tab_brow[:, HALF:]
+            left = jnp.concatenate([bc * cos - bs * sin, bs * cos_edge + bc * sin], 1).astype(jnp.bfloat16)
             maps = dot(left, right)
+            weight = tissue_ref[s, 0, c].astype(jnp.float32) / float(PATCH * PATCH)
+            base = own_rstd[s, c] * weight
+            near = maps[:, :HALF].reshape(SHIFTS // 8, 8, HALF)
+            far = maps[:, HALF:].reshape(SHIFTS // 8, 8, HALF)
             for slot in range(2):
-                piece = maps[:, slot * HALF : (slot + 1) * HALF].reshape(SHIFTS // 8, 8, HALF)
-                out[s, slot, c] = (piece * scales[slot][None]).reshape(SHIFTS, SHIFTS)
-
-    def own(s):
-        starts = [(shift_ref[s, 0, c, 0] + 64, shift_ref[s, 0, c, 1] + 64) for c in range(PC)]
-        phases = [tab_phase[shift_ref[s, 0, c, 1] + REACH] for c in range(PC)]
-        forward(img.at[s], above.at[s], below.at[s], starts, phases, tab_row, tab_col, nyq, own_spec, own_nyq, own_rstd)
-
-    for j in range(2):
-        plain(nxt.at[j], nxt_above.at[j], nxt_below.at[j], secs - 1 + j)
-
-    def local(i, carry):
-        plain(img.at[i + 1], above.at[i + 1], below.at[i + 1], i)
+                step = step_ref[slot, s].astype(jnp.float32)
+                by_near = base * rstd[s, c] * (2.0 - step)
+                by_far = base * rstd[s + 1, c] * (step - 1.0)
+                stage[s, slot, c] = (near * by_near[None] + far * by_far[None]).reshape(SHIFTS, SHIFTS)
+
+    def save(s):
+        return pltpu.make_async_copy(stage.at[s], out.at[s], out_sem.at[s])
+
+    def each(t, carry):
+        for j in range(2):
+            @pl.when(jnp.logical_and(has_next, t == 2 + j))
+            def _():
+                to_prev(j).wait_recv()
+
+                @pl.when(has_down)
+                def _():
+                    relay_down(j).start()
+
+                @pl.when(has_up)
+                def _():
+                    relay_up(j).start()
+
+        @pl.when(t < secs)
+        def _():
+            @pl.when(has_up)
+            def _():
+                to_down(t).wait_recv()
+
+            @pl.when(has_down)
+            def _():
+                to_up(t).wait_recv()
+
+            own(t)
+
+        for j in range(2):
+            @pl.when(jnp.logical_and(has_next, t == secs + j))
+            def _():
+                @pl.when(has_up)
+                def _():
+                    relay_down(j).wait_recv()
+
+                @pl.when(has_down)
+                def _():
+                    relay_up(j).wait_recv()
+
+        @pl.when(t >= 1)
+        def _():
+            plain(t)
+
+        @pl.when(t >= 2)
+        def _():
+            pairs(t - 2)
+            save(t - 2).start()
+
         return carry
 
-    lax.fori_loop(0, secs - 1, local, 0)
-
-    def each(s, carry):
-        own(s)
-        pairs(s)
-        return carry
-
-    lax.fori_loop(0, secs, each, 0)
-
-
-def from_row(block, by):
-    count = lax.axis_size("row")
-    return lax.ppermute(block, "row", [(i - by, i) for i in range(count) if 0 <= i - by < count])
-
-
-def from_next(block, by):
-    secs, rows = lax.axis_size("sec"), lax.axis_size("row")
-    pairs = [
-        ((s + 1) * rows + r - by, s * rows + r)
-        for s in range(secs - 1)
-        for r in range(rows)
-        if 0 <= r - by < rows
-    ]
-    return lax.ppermute(block, ("sec", "row"), pairs)
-
-
-def compute(image, above, below, nxt, nxt_above, nxt_below, grid_shift, partner_step, tissue):
-    secs = image.shape[0]
-    tables = [row_table(), col_tables(), back_col_tables(), back_row_tables(), phase_table()]
+    lax.fori_loop(0, secs + 2, each, 0)
+
+    @pl.when(has_prev)
+    def _():
+        for j in range(2):
+            to_prev(j).wait_send()
+
+    @pl.when(has_down)
+    def _():
+        for t in range(secs):
+            to_down(t).wait_send()
+
+    @pl.when(has_up)
+    def _():
+        for t in range(secs):
+            to_up(t).wait_send()
+
+    @pl.when(jnp.logical_and(has_next, has_down))
+    def _():
+        for j in range(2):
+            relay_down(j).wait_send()
+
+    @pl.when(jnp.logical_and(has_next, has_up))
+    def _():
+        for j in range(2):
+            relay_up(j).wait_send()
+
+    for s in range(secs):
+        save(s).wait()
+
+
+def on_device(secs_axis, rows_axis, image, grid_shift, partner_step, tissue):
+    secs, height, width = image.shape
+    tables = [jnp.asarray(t) for t in (row_table(), col_tables(), back_col_tables(), back_row_table(), col_phases(), row_phases())]
     smem = pl.BlockSpec(memory_space=pltpu.SMEM)
-    vmem = pl.BlockSpec(memory_space=pltpu.VMEM)
-    return pl.pallas_call(
-        kernel,
+    hbm = pl.BlockSpec(memory_space=pl.ANY)
+    dma = pltpu.SemaphoreType.DMA
+    maps = pl.pallas_call(
+        functools.partial(kernel, secs_axis, rows_axis),
         out_shape=jax.ShapeDtypeStruct((secs, 2, PC, SHIFTS, SHIFTS), jnp.float32),
-        in_specs=[smem] * 3 + [vmem] * 11,
-        out_specs=vmem,
-        scratch_shapes=[
+        in_specs=[smem] * 3 + [hbm] * 7,
+        out_specs=hbm,
+        scratch_shapes=[pltpu.VMEM(t.shape, t.dtype) for t in tables]
+        + [
+            pltpu.VMEM((secs + 2, height, width), jnp.bfloat16),
+            pltpu.VMEM((secs + 2, HALO, width), jnp.bfloat16),
+            pltpu.VMEM((secs + 2, HALO, width), jnp.bfloat16),
+            pltpu.VMEM((secs, 8, 4 * HALF), jnp.float32),
+            pltpu.VMEM((secs, 8, 3 * HALF), jnp.float32),
             pltpu.VMEM((16, PATCH), jnp.float32),
-            pltpu.VMEM((PC, HALF, WIDE), jnp.bfloat16),
-            pltpu.VMEM((16, WIDE), jnp.bfloat16),
-            pltpu.VMEM((PC, 8, HALF), jnp.float32),
+            pltpu.VMEM((secs, PC, HALF, WIDE), jnp.bfloat16),
+            pltpu.VMEM((secs, 16, WIDE), jnp.bfloat16),
+            pltpu.VMEM((secs, PC, 8, HALF), jnp.float32),
             pltpu.VMEM((secs + 1, PC, HALF, WIDE), jnp.bfloat16),
             pltpu.VMEM((secs + 1, 16, WIDE), jnp.bfloat16),
             pltpu.VMEM((secs + 1, PC, 8, HALF), jnp.float32),
+            pltpu.VMEM((secs, 2, PC, SHIFTS, SHIFTS), jnp.float32),
+            dma((6,)),
+            dma,
+            dma((secs,)),
+            dma((secs + 2,)),
+            dma((secs + 2,)),
+            dma((secs + 2,)),
+            dma((secs + 2,)),
+            dma((2,)),
+            dma((2,)),
         ],
-        compiler_params=pltpu.CompilerParams(vmem_limit_bytes=56 * 1024 * 1024),
+        compiler_params=pltpu.CompilerParams(
+            vmem_limit_bytes=60 * 1024 * 1024, collective_id=0, has_side_effects=True
+        ),
         cost_estimate=pl.CostEstimate(flops=6_000_000_000, bytes_accessed=8_000_000, transcendentals=0),
-    )(
-        grid_shift, partner_step, tissue, image, above, below, nxt, nxt_above, nxt_below,
-        *[jnp.asarray(t) for t in tables],
-    )
-
-
-def on_device(image, grid_shift, partner_step, tissue):
-    above = from_row(image[:, HALF - HALO :], 1)
-    below = from_row(image[:, :HALO], -1)
-    nxt = from_next(image[:2], 0)
-    nxt_above = from_next(image[:2, HALF - HALO :], 1)
-    nxt_below = from_next(image[:2, :HALO], -1)
-    maps = compute(image, above, below, nxt, nxt_above, nxt_below, grid_shift, partner_step, tissue)
-    return maps.reshape(image.shape[0], 2, 1, PC, SHIFTS * SHIFTS)
+    )(jnp.swapaxes(grid_shift, 2, 3), jnp.swapaxes(partner_step, 0, 1), tissue, image, *tables)
+    return maps.reshape(secs, 2, 1, PC, SHIFTS * SHIFTS)
 
 
 def solution(mesh):
     return jax.shard_map(
-        on_device,
+        functools.partial(on_device, mesh.shape["sec"], mesh.shape["row"]),
         mesh=mesh,
         in_specs=(
             P("sec", "row", None),

time: 52.4 us -> 34.2 us (0.65)
  the two profiles are of different devices: /device:TPU:126 before, /device:TPU:193 now
where the time goes in v2:
time: 34.2 us; the launch traced here: 34.1 us
  Pallas kernels  30.5 us (89%)
  local copies, waits for them, and re-layouts  3.53 us (10%)
    pallas_call x1, Pallas kernels, on_device(): pl.pallas_call(functools.partial(kernel, secs_axis, rows_axis), out_shape...  30.5 us
    unnamed x1, local copies, waits for them, and re-layouts  3.53 us

profile of v2, /device:TPU:193, one launch (start us, length us, event | category | flops | bytes accessed | tf_op | source)
XLA Modules:
  0.0 34.1 jit_solution(2100311065198914564)
XLA Ops:
  0.0 30.5 %shard_map.100 = f32[4,2,5,128,128]{4,3,2,1,0:T(8,128)} custom-call(s32[4,1,2,5]{3,2,1,0:T(2,128)} %bitcast.4, s32[2,4]{1,0:T(2,128)} %bitcast.5, s32[4,1,5]{2,1,0:T(1,128)} %tissue_ref.1, bf16[4,128,640]{2,1,0:T(8,128)(2,1)} %img.1, bf16[256,256]{1,0:T(8,128)(2,1)} %constant.12.clone.refs_0_, bf16[2,256,256]{2,1,0:T(8,128)(2,1)} %constant.13.clone.refs_1_, ...), custom_call_target="tpu_custom_call" | custom-call | flops 6000000000 | bytes 8000000 | tf_op jit(solution)/shard_map/pallas_call | solution.py:414
  30.5 3.5 %copy.17 = f32[4,2,1,5,16384]{4,2,3,1,0:T(1,128)} copy(f32[4,2,1,5,16384]{4,2,3,1,0:T(1,128)} %bitcast.3) | data formatting | bytes 5242880

commit v3 on v2

--- a/solution.py
+++ b/solution.py
@@ -13,6 +13,7 @@
 PATCH = 256
 HALF = 128
 REACH = 32
+GROUP = 4
 HALO = 96
 SHIFTS = 128
 WIDE = 4 * HALF
@@ -187,20 +188,29 @@
 
 def kernel(
     secs_axis, rows_axis,
-    shift_ref, step_ref, tissue_ref, img, *refs,
+    shift_hbm, step_hbm, tissue_hbm, img, *refs,
 ):
     tables, refs = refs[:6], refs[6:]
     out, refs = refs[0], refs[1:]
     tabs, refs = refs[:6], refs[6:]
     (strip, above, below, pcol, prow, nyq, own_spec, own_nyq, own_rstd, spec, spec_nyq, rstd, stage,
-     tab_sem, img_sem, out_sem, up_send, up_recv, down_send, down_recv, sec_send, sec_recv) = refs
+     tab_sem, img_sem, out_sem, up_send, up_recv, down_send, down_recv, sec_send, sec_recv,
+     transit, via_send, via_recv, shift_ref, step_ref, tissue_ref, int_sem) = refs
     tab_row, tab_col, tab_bcol, tab_brow, tab_pcol, tab_prow = tabs
     secs = own_spec.shape[0]
     sec, row = lax.axis_index("sec"), lax.axis_index("row")
     has_up, has_down = row > 0, row < rows_axis - 1
     has_prev, has_next = sec > 0, sec < secs_axis - 1
     up, down, prev, following = (sec, row - 1), (sec, row + 1), (sec - 1, row), (sec + 1, row)
-    sides = ((has_up, up), (has_down, down), (has_prev, prev), (has_next, following))
+    place = lax.rem(sec, GROUP)
+    far_send = jnp.logical_and(place == 0, has_prev)
+    carries = jnp.logical_and(place == GROUP - 1, sec >= GROUP)
+    far_take = jnp.logical_and(place == GROUP - 1, has_next)
+    via, origin, goal, carrier = [(sec + d, row) for d in (GROUP - 1, 1 - GROUP, -GROUP, GROUP)]
+    sides = (
+        (has_up, up), (has_down, down), (has_prev, prev), (has_next, following),
+        (far_send, via), (carries, origin), (carries, goal), (far_take, carrier),
+    )
 
     barrier = pltpu.get_barrier_semaphore()
     for there, where in sides:
@@ -211,6 +221,8 @@
     img_copy = pltpu.make_async_copy(img, strip.at[0:secs], img_sem)
     img_copy.start()
     loads = [pltpu.make_async_copy(t, v, tab_sem.at[i]) for i, (t, v) in enumerate(zip(tables, tabs))]
+    ints = ((shift_hbm, shift_ref), (step_hbm, step_ref), (tissue_hbm, tissue_ref))
+    loads += [pltpu.make_async_copy(h, v, int_sem.at[i]) for i, (h, v) in enumerate(ints)]
     for load in loads:
         load.start()
 
@@ -233,20 +245,36 @@
         t = secs + j
         return remote(strip.at[t, 0 : HALF // 2], below.at[t, 0 : HALF // 2], up_send.at[t], up_recv.at[t], up)
 
+    def to_via():
+        return remote(img.at[1], transit, sec_send.at[1], via_recv, via)
+
+    def onward():
+        return remote(transit, strip.at[secs + 1], via_send, sec_recv.at[1], goal)
+
+    def start_halo(t):
+        @pl.when(has_down)
+        def _():
+            to_down(t).start()
+
+        @pl.when(has_up)
+        def _():
+            to_up(t).start()
+
+    start_halo(0)
+
+    @pl.when(far_send)
+    def _():
+        to_via().start()
+
     @pl.when(has_prev)
     def _():
-        for j in range(2):
-            to_prev(j).start()
-
-    @pl.when(has_down)
-    def _():
-        for t in range(secs):
-            to_down(t).start()
-
-    @pl.when(has_up)
-    def _():
-        for t in range(secs):
-            to_up(t).start()
+        to_prev(0).start()
+
+    start_halo(1)
+
+    @pl.when(jnp.logical_and(has_prev, place > 0))
+    def _():
+        to_prev(1).start()
 
     @pl.when(jnp.logical_not(has_up))
     def _():
@@ -263,7 +291,6 @@
         below[secs:] = jnp.zeros((2, HALO, strip.shape[2]), jnp.bfloat16)
 
     nyq[...] = jnp.zeros_like(nyq)
-    img_copy.wait()
     for load in loads:
         load.wait()
 
@@ -327,6 +354,15 @@
         return pltpu.make_async_copy(stage.at[s], out.at[s], out_sem.at[s])
 
     def each(t, carry):
+        @pl.when(t + 2 < secs)
+        def _():
+            start_halo(t + 2)
+
+        @pl.when(jnp.logical_and(carries, t == 1))
+        def _():
+            to_via().wait_recv()
+            onward().start()
+
         for j in range(2):
             @pl.when(jnp.logical_and(has_next, t == 2 + j))
             def _():
@@ -374,12 +410,17 @@
 
         return carry
 
+    img_copy.wait()
     lax.fori_loop(0, secs + 2, each, 0)
 
     @pl.when(has_prev)
     def _():
         for j in range(2):
             to_prev(j).wait_send()
+
+    @pl.when(carries)
+    def _():
+        onward().wait_send()
 
     @pl.when(has_down)
     def _():
@@ -408,14 +449,13 @@
 def on_device(secs_axis, rows_axis, image, grid_shift, partner_step, tissue):
     secs, height, width = image.shape
     tables = [jnp.asarray(t) for t in (row_table(), col_tables(), back_col_tables(), back_row_table(), col_phases(), row_phases())]
-    smem = pl.BlockSpec(memory_space=pltpu.SMEM)
-    hbm = pl.BlockSpec(memory_space=pl.ANY)
+    ints = [jnp.swapaxes(grid_shift, 2, 3), jnp.swapaxes(partner_step, 0, 1), tissue]
     dma = pltpu.SemaphoreType.DMA
     maps = pl.pallas_call(
         functools.partial(kernel, secs_axis, rows_axis),
         out_shape=jax.ShapeDtypeStruct((secs, 2, PC, SHIFTS, SHIFTS), jnp.float32),
-        in_specs=[smem] * 3 + [hbm] * 7,
-        out_specs=hbm,
+        in_specs=[pl.BlockSpec(memory_space=pltpu.HBM)] * 10,
+        out_specs=pl.BlockSpec(memory_space=pl.ANY),
         scratch_shapes=[pltpu.VMEM(t.shape, t.dtype) for t in tables]
         + [
             pltpu.VMEM((secs + 2, height, width), jnp.bfloat16),
@@ -440,12 +480,21 @@
             dma((secs + 2,)),
             dma((2,)),
             dma((2,)),
+            pltpu.VMEM((height, width), jnp.bfloat16),
+            dma,
+            dma,
+        ]
+        + [pltpu.SMEM(x.shape, x.dtype) for x in ints]
+        + [
+            dma((3,)),
         ],
         compiler_params=pltpu.CompilerParams(
-            vmem_limit_bytes=60 * 1024 * 1024, collective_id=0, has_side_effects=True
+            vmem_limit_bytes=40 * 1024 * 1024, collective_id=0, has_side_effects=True
         ),
         cost_estimate=pl.CostEstimate(flops=6_000_000_000, bytes_accessed=8_000_000, transcendentals=0),
-    )(jnp.swapaxes(grid_shift, 2, 3), jnp.swapaxes(partner_step, 0, 1), tissue, image, *tables)
+    )(
+        *[pltpu.with_memory_space_constraint(x, pltpu.HBM) for x in (*ints, image, *tables)]
+    )
     return maps.reshape(secs, 2, 1, PC, SHIFTS * SHIFTS)
 
 

time: 34.2 us -> 29.1 us (0.85)
  the two profiles are of different devices: /device:TPU:193 before, /device:TPU:124 now
where the time goes in v3:
time: 29.1 us; the launch traced here: 29 us
  Pallas kernels  27.5 us (95%)
  local copies, waits for them, and re-layouts  1.49 us (5%)
    pallas_call x1, Pallas kernels, on_device(): pl.pallas_call(functools.partial(kernel, secs_axis, rows_axis), out_shape...  27.5 us
    unnamed x1, local copies, waits for them, and re-layouts  1.49 us

profile of v3, /device:TPU:124, one launch (start us, length us, event | category | flops | bytes accessed | tf_op | source)
XLA Modules:
  0.0 29.0 jit_solution(493922890350530861)
XLA Ops:
  0.0 27.5 %shard_map.100 = f32[4,2,5,128,128]{4,3,2,1,0:T(8,128)S(1)} custom-call(s32[4,1,2,5]{3,2,1,0:T(2,128)} %bitcast.4, s32[2,4]{1,0:T(2,128)} %bitcast.5, s32[4,1,5]{2,1,0:T(1,128)} %tissue_hbm.1, bf16[4,128,640]{2,1,0:T(8,128)(2,1)} %img.1, bf16[256,256]{1,0:T(8,128)(2,1)} %constant.12.clone.refs_0_, bf16[2,256,256]{2,1,0:T(8,128)(2,1)} %constant.13.clone.refs_1_, ...), custom_call_target="tpu_custom_call" | custom-call | flops 6000000000 | bytes 8000000 | tf_op jit(solution)/shard_map/pallas_call | solution.py:454
  27.5 1.5 %copy.17 = f32[4,2,1,5,16384]{4,2,3,1,0:T(1,128)} copy(f32[4,2,1,5,16384]{4,2,3,1,0:T(1,128)S(1)} %bitcast.3) | data formatting | bytes 5242880

commit v4 on v3

--- a/solution.py
+++ b/solution.py
@@ -17,6 +17,7 @@
 HALO = 96
 SHIFTS = 128
 WIDE = 4 * HALF
+STACK = PC * HALF + 16
 
 
 def angle(product):
@@ -105,78 +106,75 @@
     return jnp.concatenate([left, right], 1)
 
 
-def forward(own, above, below, starts, phases, tab_row, tab_col, nyq, spec, spec_nyq, rstd):
+def forward(jobs, tab_row, tab_col, lhs, nyq):
     first = lax.broadcasted_iota(jnp.int32, (8, HALF), 0) == 0
 
     def top(block):
         return block[0:8], block[8:]
 
-    for c in range(PC):
-        x = window(own, above, below, c, *starts[c])
-        part = dot(tab_row[...], x)
-        lo, hi = part[:, :HALF], part[:, HALF:]
-        even, odd = lo + hi, lo - hi
-        ce, se, co, so = even[:HALF], even[HALF:], odd[:HALF], odd[HALF:]
-        head, tail = top(ce)
-        centre = jnp.mean(head[0:1], axis=1, keepdims=True)
-        head = jnp.where(first, head - centre, head)
-        ce = jnp.concatenate([head, tail], 0)
-        square = jnp.zeros((8, HALF), jnp.float32)
-        edge = jnp.zeros((8, HALF), jnp.float32)
-        for block in (ce, se, co, so):
-            sq = block * block
-            square = square + jnp.sum(sq.reshape(HALF // 8, 8, HALF), axis=0)
-            edge = edge + sq[0:8]
-        total = 2.0 * square - jnp.where(first, edge, 0.0)
-        var = jnp.sum(jnp.sum(total, axis=0, keepdims=True), axis=1, keepdims=True) * (
-            HALF / float(PATCH**4)
-        )
-        rstd[c] = jnp.broadcast_to(lax.rsqrt(var + 1e-05), (8, HALF))
-        he, te = top(se)
-        ho, to = top(so)
-        nyq[c : c + 1, :HALF] = he[0:1]
-        nyq[c : c + 1, HALF:] = ho[0:1]
-        se = jnp.concatenate([jnp.where(first, 0.0, he), te], 0)
-        so = jnp.concatenate([jnp.where(first, 0.0, ho), to], 0)
-        fe = dot(jnp.concatenate([ce, se], 1).astype(jnp.bfloat16), tab_col[0])
-        fo = dot(jnp.concatenate([co, so], 1).astype(jnp.bfloat16), tab_col[1])
-        f = [fe[:, :HALF], fe[:, HALF:], fo[:, :HALF], fo[:, HALF:]]
-        if phases is not None:
-            f = turned(f, phases[c])
-        spec[c] = jnp.concatenate(f, 1).astype(jnp.bfloat16)
-    zero = jnp.zeros((16, HALF), jnp.bfloat16)
-    ne = jnp.concatenate([nyq[:, :HALF].astype(jnp.bfloat16), zero], 1)
-    no = jnp.concatenate([nyq[:, HALF:].astype(jnp.bfloat16), zero], 1)
-    fe, fo = dot(ne, tab_col[0]), dot(no, tab_col[1])
-    f = [fe[:, :HALF], fe[:, HALF:], fo[:, :HALF], fo[:, HALF:]]
-    if phases is not None:
-        rows = [jnp.concatenate([p[c] for c in range(PC)] + [jnp.zeros((16 - PC, HALF), jnp.float32)], 0) for p in zip(*[split4(q) for q in phases])]
-        f = turned(f, rows)
-    spec_nyq[...] = jnp.concatenate(f, 1).astype(jnp.bfloat16)
-
-
-def split4(p):
-    return [p[:, i * HALF : (i + 1) * HALF] for i in range(4)]
-
-
-def turned(f, phase):
-    ce, co, se, so = phase if isinstance(phase, list) else split4(phase)
-    return [
-        f[0] * ce - f[1] * se,
-        f[0] * se + f[1] * ce,
-        f[2] * co - f[3] * so,
-        f[2] * so + f[3] * co,
-    ]
+    for i, (own, above, below, starts, phases, spec, rstd) in enumerate(jobs):
+        base = i * STACK
+        for c in range(PC):
+            x = window(own, above, below, c, *starts[c])
+            part = dot(tab_row[...], x)
+            lo, hi = part[:, :HALF], part[:, HALF:]
+            even, odd = lo + hi, lo - hi
+            ce, se, co, so = even[:HALF], even[HALF:], odd[:HALF], odd[HALF:]
+            head, tail = top(ce)
+            centre = jnp.mean(head[0:1], axis=1, keepdims=True)
+            head = jnp.where(first, head - centre, head)
+            ce = jnp.concatenate([head, tail], 0)
+            square = jnp.zeros((8, HALF), jnp.float32)
+            edge = jnp.zeros((8, HALF), jnp.float32)
+            for block in (ce, se, co, so):
+                sq = block * block
+                square = square + jnp.sum(sq.reshape(HALF // 8, 8, HALF), axis=0)
+                edge = edge + sq[0:8]
+            total = 2.0 * square - jnp.where(first, edge, 0.0)
+            var = jnp.sum(jnp.sum(total, axis=0, keepdims=True), axis=1, keepdims=True) * (
+                HALF / float(PATCH**4)
+            )
+            rstd[c] = jnp.broadcast_to(lax.rsqrt(var + 1e-05), (8, HALF))
+            he, te = top(se)
+            ho, to = top(so)
+            nyq[i, c : c + 1, :HALF] = he[0:1]
+            nyq[i, c : c + 1, HALF:] = ho[0:1]
+            se = jnp.concatenate([jnp.where(first, 0.0, he), te], 0)
+            so = jnp.concatenate([jnp.where(first, 0.0, ho), to], 0)
+            rows = slice(base + c * HALF, base + (c + 1) * HALF)
+            lhs[0, rows] = jnp.concatenate([ce, se], 1).astype(jnp.bfloat16)
+            lhs[1, rows] = jnp.concatenate([co, so], 1).astype(jnp.bfloat16)
+        rows = slice(base + PC * HALF, base + STACK)
+        zero = jnp.zeros((16, HALF), jnp.bfloat16)
+        lhs[0, rows] = jnp.concatenate([nyq[i, :, :HALF].astype(jnp.bfloat16), zero], 1)
+        lhs[1, rows] = jnp.concatenate([nyq[i, :, HALF:].astype(jnp.bfloat16), zero], 1)
+    for q in range(2):
+        f = dot(lhs[q, : len(jobs) * STACK], tab_col[q])
+        for i, (_, _, _, _, phases, spec, _) in enumerate(jobs):
+            block = f[i * STACK : (i + 1) * STACK]
+            if phases is None:
+                spec[:, q * PATCH : (q + 1) * PATCH] = block.astype(jnp.bfloat16)
+                continue
+            cos = [p[:, q * HALF : (q + 1) * HALF] for p in phases]
+            sin = [p[:, (q + 2) * HALF : (q + 3) * HALF] for p in phases]
+            spare = jnp.zeros((16 - PC, HALF), jnp.float32)
+            cos.append(jnp.concatenate(cos + [spare], 0))
+            sin.append(jnp.concatenate(sin + [spare], 0))
+            for c in range(PC + 1):
+                rows = slice(c * HALF, min((c + 1) * HALF, STACK))
+                re, im = block[rows, :HALF], block[rows, HALF:]
+                turned = jnp.concatenate([re * cos[c] - im * sin[c], re * sin[c] + im * cos[c]], 1)
+                spec[rows, q * PATCH : (q + 1) * PATCH] = turned.astype(jnp.bfloat16)
 
 
 def crossed(a, b):
     out = []
     for base in (0, 2 * HALF):
         re, im = slice(base, base + HALF), slice(base + HALF, base + 2 * HALF)
-        are, aim = a[:, re].astype(jnp.float32), a[:, im].astype(jnp.float32)
-        bre, bim = b[:, re].astype(jnp.float32), b[:, im].astype(jnp.float32)
+        are, aim = a[:, re], a[:, im]
+        bre, bim = b[:, re], b[:, im]
         g = jnp.concatenate([are * bre + aim * bim, are * bim - aim * bre], 1)
-        out.append(g.astype(jnp.bfloat16))
+        out.append(g)
     return out
 
 
@@ -193,9 +191,9 @@
     tables, refs = refs[:6], refs[6:]
     out, refs = refs[0], refs[1:]
     tabs, refs = refs[:6], refs[6:]
-    (strip, above, below, pcol, prow, nyq, own_spec, own_nyq, own_rstd, spec, spec_nyq, rstd, stage,
+    (strip, above, below, pcol, prow, lhs, nyq, right, own_spec, own_rstd, spec, rstd, stage,
      tab_sem, img_sem, out_sem, up_send, up_recv, down_send, down_recv, sec_send, sec_recv,
-     transit, via_send, via_recv, shift_ref, step_ref, tissue_ref, int_sem) = refs
+     part_send, part_recv, transit, via_send, via_recv, shift_ref, step_ref, tissue_ref, int_sem) = refs
     tab_row, tab_col, tab_bcol, tab_brow, tab_pcol, tab_prow = tabs
     secs = own_spec.shape[0]
     sec, row = lax.axis_index("sec"), lax.axis_index("row")
@@ -204,13 +202,13 @@
     up, down, prev, following = (sec, row - 1), (sec, row + 1), (sec - 1, row), (sec + 1, row)
     place = lax.rem(sec, GROUP)
     far_send = jnp.logical_and(place == 0, has_prev)
-    carries = jnp.logical_and(place == GROUP - 1, sec >= GROUP)
     far_take = jnp.logical_and(place == GROUP - 1, has_next)
-    via, origin, goal, carrier = [(sec + d, row) for d in (GROUP - 1, 1 - GROUP, -GROUP, GROUP)]
-    sides = (
-        (has_up, up), (has_down, down), (has_prev, prev), (has_next, following),
-        (far_send, via), (carries, origin), (carries, goal), (far_take, carrier),
-    )
+    carries = [jnp.logical_and(place == p, sec > p) for p in range(GROUP)]
+    sides = [(has_up, up), (has_down, down), (has_prev, prev), (has_next, following)]
+    for p in range(1, GROUP):
+        if p > 1:
+            sides += [(far_send, (sec + p, row)), (carries[p], (sec - p, row))]
+        sides += [(far_take, (sec + p + 1, row)), (carries[p], (sec - p - 1, row))]
 
     barrier = pltpu.get_barrier_semaphore()
     for there, where in sides:
@@ -245,11 +243,23 @@
         t = secs + j
         return remote(strip.at[t, 0 : HALF // 2], below.at[t, 0 : HALF // 2], up_send.at[t], up_recv.at[t], up)
 
-    def to_via():
-        return remote(img.at[1], transit, sec_send.at[1], via_recv, via)
-
-    def onward():
-        return remote(transit, strip.at[secs + 1], via_send, sec_recv.at[1], goal)
+    def part(p):
+        return p // 2, slice(p % 2 * (HALF // 2), (p % 2 + 1) * (HALF // 2))
+
+    def to_far():
+        return remote(img.at[0, : HALF // 2], strip.at[secs, : HALF // 2], part_send.at[0], part_recv.at[0], prev)
+
+    def to_carrier(p):
+        j, rows = part(p)
+        return remote(img.at[j, rows], transit, part_send.at[p], via_recv, (sec + p, row))
+
+    def onward(p):
+        j, rows = part(p)
+        return remote(transit, strip.at[secs + j, rows], via_send, part_recv.at[p], (sec - p - 1, row))
+
+    def arrival(p):
+        j, rows = part(p)
+        return remote(transit, strip.at[secs + j, rows], via_send, part_recv.at[p], (sec + p + 1, row))
 
     def start_halo(t):
         @pl.when(has_down)
@@ -262,17 +272,22 @@
 
     start_halo(0)
 
+    near_send = jnp.logical_and(has_prev, place > 0)
+    near_take = jnp.logical_and(has_next, place < GROUP - 1)
+
     @pl.when(far_send)
     def _():
-        to_via().start()
-
-    @pl.when(has_prev)
+        for p in range(1, GROUP):
+            to_carrier(p).start()
+        to_far().start()
+
+    @pl.when(near_send)
     def _():
         to_prev(0).start()
 
     start_halo(1)
 
-    @pl.when(jnp.logical_and(has_prev, place > 0))
+    @pl.when(near_send)
     def _():
         to_prev(1).start()
 
@@ -306,40 +321,36 @@
         phase[...] = picked.reshape(secs, 8, picked.shape[1])
 
     def plain(t):
-        forward(
-            strip.at[t], above.at[t], below.at[t], [(None, 64)] * PC, None, tab_row, tab_col, nyq,
-            spec.at[t - 1], spec_nyq.at[t - 1], rstd.at[t - 1],
-        )
+        return (strip.at[t], above.at[t], below.at[t], [(None, 64)] * PC, None, spec.at[t - 1], rstd.at[t - 1])
 
     def own(s):
         starts = [(shift_ref[s, 0, 0, c] + 64, shift_ref[s, 0, 1, c] + 64) for c in range(PC)]
         phases = [pcol[s, c : c + 1] for c in range(PC)]
-        forward(
-            strip.at[s], above.at[s], below.at[s], starts, phases, tab_row, tab_col, nyq,
-            own_spec.at[s], own_nyq.at[s], own_rstd.at[s],
-        )
+        return (strip.at[s], above.at[s], below.at[s], starts, phases, own_spec.at[s], own_rstd.at[s])
+
+    def spectra(*jobs):
+        forward(jobs, tab_row, tab_col, lhs, nyq)
 
     first = lax.broadcasted_iota(jnp.int32, (8, HALF), 0) == 0
 
     def pairs(s):
+        for part in range(2):
+            ge, go = crossed(own_spec[s], spec[s + part])
+            g = dot(ge, tab_bcol[0]) + dot(go, tab_bcol[1])
+            lanes = slice(part * HALF, (part + 1) * HALF)
+            for c in range(PC):
+                block = g[c * HALF : (c + 1) * HALF]
+                edge = jnp.broadcast_to(g[PC * HALF + c : PC * HALF + c + 1, :HALF], (8, HALF))
+                im = block[:, HALF:]
+                im = jnp.concatenate([jnp.where(first, edge, im[0:8]), im[8:]], 0)
+                right[c, :HALF, lanes] = block[:, :HALF].astype(jnp.bfloat16)
+                right[c, HALF:, lanes] = im.astype(jnp.bfloat16)
         for c in range(PC):
-            cols = []
-            for part in (s, s + 1):
-                ge, go = crossed(own_spec[s, c], spec[part, c])
-                xe, xo = crossed(own_nyq[s], spec_nyq[part])
-                ge = jnp.concatenate([ge, xe], 0)
-                go = jnp.concatenate([go, xo], 0)
-                g = dot(ge, tab_bcol[0]) + dot(go, tab_bcol[1])
-                edge = jnp.broadcast_to(g[HALF + c : HALF + c + 1, :HALF], (8, HALF))
-                im = g[:HALF, HALF:]
-                head = jnp.where(first, edge, im[0:8])
-                cols.append(jnp.concatenate([g[:HALF, :HALF], head, im[8:]], 0))
-            right = jnp.concatenate(cols, 1).astype(jnp.bfloat16)
             turn = prow[s, c : c + 1]
             cos, cos_edge, sin = turn[:, :HALF], turn[:, HALF : 2 * HALF], turn[:, 2 * HALF :]
             bc, bs = tab_brow[:, :HALF], tab_brow[:, HALF:]
             left = jnp.concatenate([bc * cos - bs * sin, bs * cos_edge + bc * sin], 1).astype(jnp.bfloat16)
-            maps = dot(left, right)
+            maps = dot(left, right[c])
             weight = tissue_ref[s, 0, c].astype(jnp.float32) / float(PATCH * PATCH)
             base = own_rstd[s, c] * weight
             near = maps[:, :HALF].reshape(SHIFTS // 8, 8, HALF)
@@ -358,16 +369,24 @@
         def _():
             start_halo(t + 2)
 
-        @pl.when(jnp.logical_and(carries, t == 1))
-        def _():
-            to_via().wait_recv()
-            onward().start()
+        for p in range(1, GROUP):
+            @pl.when(jnp.logical_and(carries[p], t == 1))
+            def _():
+                to_carrier(p).wait_recv()
+                onward(p).start()
 
         for j in range(2):
-            @pl.when(jnp.logical_and(has_next, t == 2 + j))
+            @pl.when(jnp.logical_and(near_take, t == 3 + j))
             def _():
                 to_prev(j).wait_recv()
 
+            @pl.when(jnp.logical_and(far_take, t == 3 + j))
+            def _():
+                arrival(2 * j).wait_recv()
+                arrival(2 * j + 1).wait_recv()
+
+            @pl.when(jnp.logical_and(has_next, t == 3 + j))
+            def _():
                 @pl.when(has_down)
                 def _():
                     relay_down(j).start()
@@ -386,8 +405,6 @@
             def _():
                 to_up(t).wait_recv()
 
-            own(t)
-
         for j in range(2):
             @pl.when(jnp.logical_and(has_next, t == secs + j))
             def _():
@@ -399,9 +416,17 @@
                 def _():
                     relay_up(j).wait_recv()
 
-        @pl.when(t >= 1)
-        def _():
-            plain(t)
+        @pl.when(t == 0)
+        def _():
+            spectra(own(t))
+
+        @pl.when(jnp.logical_and(t >= 1, t < secs))
+        def _():
+            spectra(own(t), plain(t))
+
+        @pl.when(t >= secs)
+        def _():
+            spectra(plain(t))
 
         @pl.when(t >= 2)
         def _():
@@ -413,14 +438,21 @@
     img_copy.wait()
     lax.fori_loop(0, secs + 2, each, 0)
 
-    @pl.when(has_prev)
+    @pl.when(near_send)
     def _():
         for j in range(2):
             to_prev(j).wait_send()
 
-    @pl.when(carries)
-    def _():
-        onward().wait_send()
+    @pl.when(far_send)
+    def _():
+        to_far().wait_send()
+        for p in range(1, GROUP):
+            to_carrier(p).wait_send()
+
+    for p in range(1, GROUP):
+        @pl.when(carries[p])
+        def _():
+            onward(p).wait_send()
 
     @pl.when(has_down)
     def _():
@@ -463,12 +495,12 @@
             pltpu.VMEM((secs + 2, HALO, width), jnp.bfloat16),
             pltpu.VMEM((secs, 8, 4 * HALF), jnp.float32),
             pltpu.VMEM((secs, 8, 3 * HALF), jnp.float32),
-            pltpu.VMEM((16, PATCH), jnp.float32),
-            pltpu.VMEM((secs, PC, HALF, WIDE), jnp.bfloat16),
-            pltpu.VMEM((secs, 16, WIDE), jnp.bfloat16),
+            pltpu.VMEM((2, 2 * STACK, PATCH), jnp.bfloat16),
+            pltpu.VMEM((2, 16, PATCH), jnp.float32),
+            pltpu.VMEM((PC, PATCH, PATCH), jnp.bfloat16),
+            pltpu.VMEM((secs, STACK, WIDE), jnp.bfloat16),
             pltpu.VMEM((secs, PC, 8, HALF), jnp.float32),
-            pltpu.VMEM((secs + 1, PC, HALF, WIDE), jnp.bfloat16),
-            pltpu.VMEM((secs + 1, 16, WIDE), jnp.bfloat16),
+            pltpu.VMEM((secs + 1, STACK, WIDE), jnp.bfloat16),
             pltpu.VMEM((secs + 1, PC, 8, HALF), jnp.float32),
             pltpu.VMEM((secs, 2, PC, SHIFTS, SHIFTS), jnp.float32),
             dma((6,)),
@@ -480,7 +512,9 @@
             dma((secs + 2,)),
             dma((2,)),
             dma((2,)),
-            pltpu.VMEM((height, width), jnp.bfloat16),
+            dma((GROUP,)),
+            dma((GROUP,)),
+            pltpu.VMEM((HALF // 2, width), jnp.bfloat16),
             dma,
             dma,
         ]

time: 29.1 us -> 24.5 us (0.84)
  the two profiles are of different devices: /device:TPU:124 before, /device:TPU:193 now
where the time goes in v4:
time: 24.5 us; the launch traced here: 24.4 us
  Pallas kernels  22.9 us (93%)
  local copies, waits for them, and re-layouts  1.49 us (6%)
    pallas_call x1, Pallas kernels, on_device(): pl.pallas_call(functools.partial(kernel, secs_axis, rows_axis), out_shape...  22.9 us
    unnamed x1, local copies, waits for them, and re-layouts  1.49 us

profile of v4, /device:TPU:193, one launch (start us, length us, event | category | flops | bytes accessed | tf_op | source)
XLA Modules:
  0.0 24.4 jit_solution(16943117339302114315)
XLA Ops:
  0.0 22.9 %shard_map.100 = f32[4,2,5,128,128]{4,3,2,1,0:T(8,128)S(1)} custom-call(s32[4,1,2,5]{3,2,1,0:T(2,128)} %bitcast.4, s32[2,4]{1,0:T(2,128)} %bitcast.5, s32[4,1,5]{2,1,0:T(1,128)} %tissue_hbm.1, bf16[4,128,640]{2,1,0:T(8,128)(2,1)} %img.1, bf16[256,256]{1,0:T(8,128)(2,1)} %constant.12.clone.refs_0_, bf16[2,256,256]{2,1,0:T(8,128)(2,1)} %constant.13.clone.refs_1_, ...), custom_call_target="tpu_custom_call" | custom-call | flops 6000000000 | bytes 8000000 | tf_op jit(solution)/shard_map/pallas_call | solution.py:486
  22.9 1.5 %copy.17 = f32[4,2,1,5,16384]{4,2,3,1,0:T(1,128)} copy(f32[4,2,1,5,16384]{4,2,3,1,0:T(1,128)S(1)} %bitcast.3) | data formatting | bytes 5242880

commit v5 on v4

--- a/solution.py
+++ b/solution.py
@@ -285,11 +285,16 @@
     def _():
         to_prev(0).start()
 
-    start_halo(1)
+    for t in range(1, secs - 1):
+        start_halo(t)
 
     @pl.when(near_send)
     def _():
         to_prev(1).start()
+
+    @pl.when(jnp.logical_not(jnp.logical_or(jnp.logical_or(carries[1], carries[2]), carries[3])))
+    def _():
+        start_halo(secs - 1)
 
     @pl.when(jnp.logical_not(has_up))
     def _():
@@ -364,36 +369,35 @@
     def save(s):
         return pltpu.make_async_copy(stage.at[s], out.at[s], out_sem.at[s])
 
+    def take(t, cases):
+        for there, j, when in cases:
+            @pl.when(jnp.logical_and(there, t == when))
+            def _():
+                if there is near_take:
+                    to_prev(j).wait_recv()
+                else:
+                    arrival(2 * j).wait_recv()
+
+                @pl.when(has_up)
+                def _():
+                    relay_up(j).start()
+
+                if there is not near_take:
+                    arrival(2 * j + 1).wait_recv()
+
+                @pl.when(has_down)
+                def _():
+                    relay_down(j).start()
+
     def each(t, carry):
-        @pl.when(t + 2 < secs)
-        def _():
-            start_halo(t + 2)
-
         for p in range(1, GROUP):
-            @pl.when(jnp.logical_and(carries[p], t == 1))
+            @pl.when(jnp.logical_and(carries[p], t == 0))
             def _():
                 to_carrier(p).wait_recv()
                 onward(p).start()
-
-        for j in range(2):
-            @pl.when(jnp.logical_and(near_take, t == 3 + j))
-            def _():
-                to_prev(j).wait_recv()
-
-            @pl.when(jnp.logical_and(far_take, t == 3 + j))
-            def _():
-                arrival(2 * j).wait_recv()
-                arrival(2 * j + 1).wait_recv()
-
-            @pl.when(jnp.logical_and(has_next, t == 3 + j))
-            def _():
-                @pl.when(has_down)
-                def _():
-                    relay_down(j).start()
-
-                @pl.when(has_up)
-                def _():
-                    relay_up(j).start()
+                start_halo(secs - 1)
+
+        take(t, ((far_take, 0, 3),))
 
         @pl.when(t < secs)
         def _():
@@ -427,6 +431,8 @@
         @pl.when(t >= secs)
         def _():
             spectra(plain(t))
+
+        take(t, ((near_take, 0, 2), (near_take, 1, 3), (far_take, 1, 3)))
 
         @pl.when(t >= 2)
         def _():

time: 24.5 us -> 23.5 us (0.959)
  Pallas kernels: 22.9 us -> 21.9 us
    pallas_call x1, Pallas kernels: 22.9 us -> 21.9 us  [on_device(): pl.pallas_call(functools.partial(kernel, secs_axis, rows_axis), out_shape...]
where the time goes in v5:
time: 23.5 us; the launch traced here: 23.4 us
  Pallas kernels  21.9 us (93%)
  local copies, waits for them, and re-layouts  1.49 us (6%)
    pallas_call x1, Pallas kernels, on_device(): pl.pallas_call(functools.partial(kernel, secs_axis, rows_axis), out_shape...  21.9 us
    unnamed x1, local copies, waits for them, and re-layouts  1.49 us

profile of v5, /device:TPU:193, one launch (start us, length us, event | category | flops | bytes accessed | tf_op | source)
XLA Modules:
  0.0 23.4 jit_solution(8217049953799933615)
XLA Ops:
  0.0 21.9 %shard_map.100 = f32[4,2,5,128,128]{4,3,2,1,0:T(8,128)S(1)} custom-call(s32[4,1,2,5]{3,2,1,0:T(2,128)} %bitcast.4, s32[2,4]{1,0:T(2,128)} %bitcast.5, s32[4,1,5]{2,1,0:T(1,128)} %tissue_hbm.1, bf16[4,128,640]{2,1,0:T(8,128)(2,1)} %img.1, bf16[256,256]{1,0:T(8,128)(2,1)} %constant.12.clone.refs_0_, bf16[2,256,256]{2,1,0:T(8,128)(2,1)} %constant.13.clone.refs_1_, ...), custom_call_target="tpu_custom_call" | custom-call | flops 6000000000 | bytes 8000000 | tf_op jit(solution)/shard_map/pallas_call | solution.py:492
  21.9 1.5 %copy.17 = f32[4,2,1,5,16384]{4,2,3,1,0:T(1,128)} copy(f32[4,2,1,5,16384]{4,2,3,1,0:T(1,128)S(1)} %bitcast.3) | data formatting | bytes 5242880

commit v6 on v5

--- a/solution.py
+++ b/solution.py
@@ -369,80 +369,92 @@
     def save(s):
         return pltpu.make_async_copy(stage.at[s], out.at[s], out_sem.at[s])
 
-    def take(t, cases):
-        for there, j, when in cases:
-            @pl.when(jnp.logical_and(there, t == when))
+    def pass_on(j):
+        @pl.when(has_up)
+        def _():
+            relay_up(j).start()
+
+        @pl.when(has_down)
+        def _():
+            relay_down(j).start()
+
+    def wait_halo(t):
+        @pl.when(has_up)
+        def _():
+            to_down(t).wait_recv()
+
+        @pl.when(has_down)
+        def _():
+            to_up(t).wait_recv()
+
+    def far_pass(j):
+        arrival(2 * j).wait_recv()
+
+        @pl.when(has_up)
+        def _():
+            relay_up(j).start()
+
+        arrival(2 * j + 1).wait_recv()
+
+        @pl.when(has_down)
+        def _():
+            relay_down(j).start()
+
+    def near_pass(j):
+        to_prev(j).wait_recv()
+        pass_on(j)
+
+    def early(t, carry):
+        @pl.when(jnp.logical_and(far_take, t == 3))
+        def _():
+            far_pass(0)
+
+        wait_halo(t)
+        spectra(own(t), plain(t))
+
+        @pl.when(t >= 2)
+        def _():
+            @pl.when(near_take)
             def _():
-                if there is near_take:
-                    to_prev(j).wait_recv()
-                else:
-                    arrival(2 * j).wait_recv()
-
-                @pl.when(has_up)
-                def _():
-                    relay_up(j).start()
-
-                if there is not near_take:
-                    arrival(2 * j + 1).wait_recv()
-
-                @pl.when(has_down)
-                def _():
-                    relay_down(j).start()
-
-    def each(t, carry):
-        for p in range(1, GROUP):
-            @pl.when(jnp.logical_and(carries[p], t == 0))
+                near_pass(t - 2)
+
+            @pl.when(jnp.logical_and(far_take, t == 3))
             def _():
-                to_carrier(p).wait_recv()
-                onward(p).start()
-                start_halo(secs - 1)
-
-        take(t, ((far_take, 0, 3),))
-
-        @pl.when(t < secs)
+                far_pass(1)
+
+            pairs(t - 2)
+            save(t - 2).start()
+
+        return carry
+
+    def late(t, carry):
+        @pl.when(has_next)
         def _():
             @pl.when(has_up)
             def _():
-                to_down(t).wait_recv()
+                relay_down(t - secs).wait_recv()
 
             @pl.when(has_down)
             def _():
-                to_up(t).wait_recv()
-
-        for j in range(2):
-            @pl.when(jnp.logical_and(has_next, t == secs + j))
-            def _():
-                @pl.when(has_up)
-                def _():
-                    relay_down(j).wait_recv()
-
-                @pl.when(has_down)
-                def _():
-                    relay_up(j).wait_recv()
-
-        @pl.when(t == 0)
-        def _():
-            spectra(own(t))
-
-        @pl.when(jnp.logical_and(t >= 1, t < secs))
-        def _():
-            spectra(own(t), plain(t))
-
-        @pl.when(t >= secs)
-        def _():
-            spectra(plain(t))
-
-        take(t, ((near_take, 0, 2), (near_take, 1, 3), (far_take, 1, 3)))
-
-        @pl.when(t >= 2)
-        def _():
-            pairs(t - 2)
-            save(t - 2).start()
-
+                relay_up(t - secs).wait_recv()
+
+        spectra(plain(t))
+        pairs(t - 2)
+        save(t - 2).start()
         return carry
 
+    for p in range(1, GROUP):
+        @pl.when(carries[p])
+        def _():
+            to_carrier(p).wait_recv()
+            onward(p).start()
+            start_halo(secs - 1)
+
     img_copy.wait()
-    lax.fori_loop(0, secs + 2, each, 0)
+    wait_halo(0)
+    spectra(own(0))
+    lax.fori_loop(1, secs, early, 0)
+    lax.fori_loop(secs, secs + 2, late, 0)
 
     @pl.when(near_send)
     def _():

time: 23.5 us -> 23.3 us (level)
  no operation moved by 1% of the time
where the time goes in v6:
time: 23.3 us; the launch traced here: 23.2 us
  Pallas kernels  21.7 us (93%)
  local copies, waits for them, and re-layouts  1.49 us (6%)
    pallas_call x1, Pallas kernels, on_device(): pl.pallas_call(functools.partial(kernel, secs_axis, rows_axis), out_shape...  21.7 us
    unnamed x1, local copies, waits for them, and re-layouts  1.49 us

profile of v6, /device:TPU:193, one launch (start us, length us, event | category | flops | bytes accessed | tf_op | source)
XLA Modules:
  0.0 23.2 jit_solution(9338118021277612888)
XLA Ops:
  0.0 21.7 %shard_map.100 = f32[4,2,5,128,128]{4,3,2,1,0:T(8,128)S(1)} custom-call(s32[4,1,2,5]{3,2,1,0:T(2,128)} %bitcast.4, s32[2,4]{1,0:T(2,128)} %bitcast.5, s32[4,1,5]{2,1,0:T(1,128)} %tissue_hbm.1, bf16[4,128,640]{2,1,0:T(8,128)(2,1)} %img.1, bf16[256,256]{1,0:T(8,128)(2,1)} %constant.12.clone.refs_0_, bf16[2,256,256]{2,1,0:T(8,128)(2,1)} %constant.13.clone.refs_1_, ...), custom_call_target="tpu_custom_call" | custom-call | flops 6000000000 | bytes 8000000 | tf_op jit(solution)/shard_map/pallas_call | solution.py:504
  21.7 1.5 %copy.17 = f32[4,2,1,5,16384]{4,2,3,1,0:T(1,128)} copy(f32[4,2,1,5,16384]{4,2,3,1,0:T(1,128)S(1)} %bitcast.3) | data formatting | bytes 5242880

commit v7 on v6

--- a/solution.py
+++ b/solution.py
@@ -193,7 +193,7 @@
     tabs, refs = refs[:6], refs[6:]
     (strip, above, below, pcol, prow, lhs, nyq, right, own_spec, own_rstd, spec, rstd, stage,
      tab_sem, img_sem, out_sem, up_send, up_recv, down_send, down_recv, sec_send, sec_recv,
-     part_send, part_recv, transit, via_send, via_recv, shift_ref, step_ref, tissue_ref, int_sem) = refs
+     part_send, part_recv, transit, via_send, via_recv, ready, shift_ref, step_ref, tissue_ref, int_sem) = refs
     tab_row, tab_col, tab_bcol, tab_brow, tab_pcol, tab_prow = tabs
     secs = own_spec.shape[0]
     sec, row = lax.axis_index("sec"), lax.axis_index("row")
@@ -204,14 +204,16 @@
     far_send = jnp.logical_and(place == 0, has_prev)
     far_take = jnp.logical_and(place == GROUP - 1, has_next)
     carries = [jnp.logical_and(place == p, sec > p) for p in range(GROUP)]
-    sides = [(has_up, up), (has_down, down), (has_prev, prev), (has_next, following)]
-    for p in range(1, GROUP):
-        if p > 1:
-            sides += [(far_send, (sec + p, row)), (carries[p], (sec - p, row))]
-        sides += [(far_take, (sec + p + 1, row)), (carries[p], (sec - p - 1, row))]
+    near_send = jnp.logical_and(has_prev, place > 0)
+    near_take = jnp.logical_and(has_next, place < GROUP - 1)
+    sides = [(has_up, up), (has_down, down), (near_send, prev), (near_take, following)]
+    for p in range(2, GROUP):
+        sides += [(far_send, (sec + p, row)), (carries[p], (sec - p, row))]
+    greeted = [(far_send, prev)] + [(carries[p], (sec - p - 1, row)) for p in range(1, GROUP)]
+    expected = sum(there.astype(jnp.int32) for there, _ in sides) + GROUP * far_take.astype(jnp.int32)
 
     barrier = pltpu.get_barrier_semaphore()
-    for there, where in sides:
+    for there, where in sides + greeted:
         @pl.when(there)
         def _():
             pl.semaphore_signal(barrier, inc=1, device_id=where, device_id_type=pl.DeviceIdType.MESH)
@@ -224,7 +226,12 @@
     for load in loads:
         load.start()
 
-    pl.semaphore_wait(barrier, sum(there.astype(jnp.int32) for there, _ in sides))
+    pl.semaphore_wait(barrier, expected)
+
+    @pl.when(far_take)
+    def _():
+        for p in range(GROUP):
+            pl.semaphore_signal(ready, inc=1, device_id=(sec + p + 1, row), device_id_type=pl.DeviceIdType.MESH)
 
     def to_prev(j):
         return remote(img.at[j], strip.at[secs + j], sec_send.at[j], sec_recv.at[j], prev)
@@ -272,14 +279,10 @@
 
     start_halo(0)
 
-    near_send = jnp.logical_and(has_prev, place > 0)
-    near_take = jnp.logical_and(has_next, place < GROUP - 1)
-
     @pl.when(far_send)
     def _():
         for p in range(1, GROUP):
             to_carrier(p).start()
-        to_far().start()
 
     @pl.when(near_send)
     def _():
@@ -295,6 +298,11 @@
     @pl.when(jnp.logical_not(jnp.logical_or(jnp.logical_or(carries[1], carries[2]), carries[3])))
     def _():
         start_halo(secs - 1)
+
+    @pl.when(far_send)
+    def _():
+        pl.semaphore_wait(ready, 1)
+        to_far().start()
 
     @pl.when(jnp.logical_not(has_up))
     def _():
@@ -405,10 +413,6 @@
         pass_on(j)
 
     def early(t, carry):
-        @pl.when(jnp.logical_and(far_take, t == 3))
-        def _():
-            far_pass(0)
-
         wait_halo(t)
         spectra(own(t), plain(t))
 
@@ -420,7 +424,7 @@
 
             @pl.when(jnp.logical_and(far_take, t == 3))
             def _():
-                far_pass(1)
+                far_pass(0)
 
             pairs(t - 2)
             save(t - 2).start()
@@ -446,6 +450,7 @@
     for p in range(1, GROUP):
         @pl.when(carries[p])
         def _():
+            pl.semaphore_wait(ready, 1)
             to_carrier(p).wait_recv()
             onward(p).start()
             start_halo(secs - 1)
@@ -454,6 +459,11 @@
     wait_halo(0)
     spectra(own(0))
     lax.fori_loop(1, secs, early, 0)
+
+    @pl.when(far_take)
+    def _():
+        far_pass(1)
+
     lax.fori_loop(secs, secs + 2, late, 0)
 
     @pl.when(near_send)
@@ -535,6 +545,7 @@
             pltpu.VMEM((HALF // 2, width), jnp.bfloat16),
             dma,
             dma,
+            pltpu.SemaphoreType.REGULAR,
         ]
         + [pltpu.SMEM(x.shape, x.dtype) for x in ints]
         + [

time: 23.3 us -> 25 us (1.073)
  the two profiles are of different devices: /device:TPU:193 before, /device:TPU:125 now
where the time goes in v7:
time: 25 us; the launch traced here: 24.9 us
  Pallas kernels  23.4 us (94%)
  local copies, waits for them, and re-layouts  1.49 us (6%)
    pallas_call x1, Pallas kernels, on_device(): pl.pallas_call(functools.partial(kernel, secs_axis, rows_axis), out_shape...  23.4 us
    unnamed x1, local copies, waits for them, and re-layouts  1.49 us

profile of v7, /device:TPU:125, one launch (start us, length us, event | category | flops | bytes accessed | tf_op | source)
XLA Modules:
  0.0 24.9 jit_solution(5201420568563098338)
XLA Ops:
  0.0 23.4 %shard_map.100 = f32[4,2,5,128,128]{4,3,2,1,0:T(8,128)S(1)} custom-call(s32[4,1,2,5]{3,2,1,0:T(2,128)} %bitcast.4, s32[2,4]{1,0:T(2,128)} %bitcast.5, s32[4,1,5]{2,1,0:T(1,128)} %tissue_hbm.1, bf16[4,128,640]{2,1,0:T(8,128)(2,1)} %img.1, bf16[256,256]{1,0:T(8,128)(2,1)} %constant.12.clone.refs_0_, bf16[2,256,256]{2,1,0:T(8,128)(2,1)} %constant.13.clone.refs_1_, ...), custom_call_target="tpu_custom_call" | custom-call | flops 6000000000 | bytes 8000000 | tf_op jit(solution)/shard_map/pallas_call | solution.py:514
  23.4 1.5 %copy.17 = f32[4,2,1,5,16384]{4,2,3,1,0:T(1,128)} copy(f32[4,2,1,5,16384]{4,2,3,1,0:T(1,128)S(1)} %bitcast.3) | data formatting | bytes 5242880

commit v8 on v7

--- a/solution.py
+++ b/solution.py
@@ -193,7 +193,7 @@
     tabs, refs = refs[:6], refs[6:]
     (strip, above, below, pcol, prow, lhs, nyq, right, own_spec, own_rstd, spec, rstd, stage,
      tab_sem, img_sem, out_sem, up_send, up_recv, down_send, down_recv, sec_send, sec_recv,
-     part_send, part_recv, transit, via_send, via_recv, ready, shift_ref, step_ref, tissue_ref, int_sem) = refs
+     part_send, part_recv, transit, via_send, via_recv, slant_send, ready, shift_ref, step_ref, tissue_ref, int_sem) = refs
     tab_row, tab_col, tab_bcol, tab_brow, tab_pcol, tab_prow = tabs
     secs = own_spec.shape[0]
     sec, row = lax.axis_index("sec"), lax.axis_index("row")
@@ -210,6 +210,9 @@
     for p in range(2, GROUP):
         sides += [(far_send, (sec + p, row)), (carries[p], (sec - p, row))]
     greeted = [(far_send, prev)] + [(carries[p], (sec - p - 1, row)) for p in range(1, GROUP)]
+    odd = lax.rem(row, 2) == 1
+    edge_up = jnp.logical_and(jnp.logical_not(odd), has_up)
+    edge_down = jnp.logical_and(odd, has_down)
     expected = sum(there.astype(jnp.int32) for there, _ in sides) + GROUP * far_take.astype(jnp.int32)
 
     barrier = pltpu.get_barrier_semaphore()
@@ -264,6 +267,15 @@
         j, rows = part(p)
         return remote(transit, strip.at[secs + j, rows], via_send, part_recv.at[p], (sec - p - 1, row))
 
+    def slant(p):
+        t, source = secs + p // 2, img.at[0, : HALF // 2] if p == 0 else transit
+        if p % 2 == 0:
+            return remote(source, below.at[t, 0 : HALF // 2], slant_send, up_recv.at[t], (sec - p - 1, row - 1))
+        return remote(source, above.at[t, HALO - HALF // 2 : HALO], slant_send, down_recv.at[t], (sec - p - 1, row + 1))
+
+    def slants(p):
+        return jnp.logical_and(far_send if p == 0 else carries[p], edge_down if p % 2 else edge_up)
+
     def arrival(p):
         j, rows = part(p)
         return remote(transit, strip.at[secs + j, rows], via_send, part_recv.at[p], (sec + p + 1, row))
@@ -303,6 +315,10 @@
     def _():
         pl.semaphore_wait(ready, 1)
         to_far().start()
+
+    @pl.when(slants(0))
+    def _():
+        slant(0).start()
 
     @pl.when(jnp.logical_not(has_up))
     def _():
@@ -398,13 +414,13 @@
     def far_pass(j):
         arrival(2 * j).wait_recv()
 
-        @pl.when(has_up)
+        @pl.when(jnp.logical_and(has_up, jnp.logical_not(edge_up)))
         def _():
             relay_up(j).start()
 
         arrival(2 * j + 1).wait_recv()
 
-        @pl.when(has_down)
+        @pl.when(jnp.logical_and(has_down, jnp.logical_not(edge_down)))
         def _():
             relay_down(j).start()
 
@@ -453,6 +469,13 @@
             pl.semaphore_wait(ready, 1)
             to_carrier(p).wait_recv()
             onward(p).start()
+
+        @pl.when(slants(p))
+        def _():
+            slant(p).start()
+
+        @pl.when(carries[p])
+        def _():
             start_halo(secs - 1)
 
     img_copy.wait()
@@ -492,12 +515,20 @@
         for t in range(secs):
             to_up(t).wait_send()
 
-    @pl.when(jnp.logical_and(has_next, has_down))
+    for p in range(GROUP):
+        @pl.when(slants(p))
+        def _():
+            slant(p).wait_send()
+
+    left_down = jnp.logical_not(jnp.logical_and(far_take, edge_down))
+    left_up = jnp.logical_not(jnp.logical_and(far_take, edge_up))
+
+    @pl.when(jnp.logical_and(jnp.logical_and(has_next, has_down), left_down))
     def _():
         for j in range(2):
             relay_down(j).wait_send()
 
-    @pl.when(jnp.logical_and(has_next, has_up))
+    @pl.when(jnp.logical_and(jnp.logical_and(has_next, has_up), left_up))
     def _():
         for j in range(2):
             relay_up(j).wait_send()
@@ -545,6 +576,7 @@
             pltpu.VMEM((HALF // 2, width), jnp.bfloat16),
             dma,
             dma,
+            dma,
             pltpu.SemaphoreType.REGULAR,
         ]
         + [pltpu.SMEM(x.shape, x.dtype) for x in ints]

time: 25 us -> 23.9 us (0.956)
  the two profiles are of different devices: /device:TPU:125 before, /device:TPU:127 now
where the time goes in v8:
time: 23.9 us; the launch traced here: 23.8 us
  Pallas kernels  22.3 us (93%)
  local copies, waits for them, and re-layouts  1.49 us (6%)
    pallas_call x1, Pallas kernels, on_device(): pl.pallas_call(functools.partial(kernel, secs_axis, rows_axis), out_shape...  22.3 us
    unnamed x1, local copies, waits for them, and re-layouts  1.49 us

profile of v8, /device:TPU:127, one launch (start us, length us, event | category | flops | bytes accessed | tf_op | source)
XLA Modules:
  0.0 23.8 jit_solution(13853806598499357157)
XLA Ops:
  0.0 22.3 %shard_map.100 = f32[4,2,5,128,128]{4,3,2,1,0:T(8,128)S(1)} custom-call(s32[4,1,2,5]{3,2,1,0:T(2,128)} %bitcast.4, s32[2,4]{1,0:T(2,128)} %bitcast.5, s32[4,1,5]{2,1,0:T(1,128)} %tissue_hbm.1, bf16[4,128,640]{2,1,0:T(8,128)(2,1)} %img.1, bf16[256,256]{1,0:T(8,128)(2,1)} %constant.12.clone.refs_0_, bf16[2,256,256]{2,1,0:T(8,128)(2,1)} %constant.13.clone.refs_1_, ...), custom_call_target="tpu_custom_call" | custom-call | flops 6000000000 | bytes 8000000 | tf_op jit(solution)/shard_map/pallas_call | solution.py:545
  22.3 1.5 %copy.17 = f32[4,2,1,5,16384]{4,2,3,1,0:T(1,128)} copy(f32[4,2,1,5,16384]{4,2,3,1,0:T(1,128)S(1)} %bitcast.3) | data formatting | bytes 5242880

commit v9 on v8

--- a/solution.py
+++ b/solution.py
@@ -412,17 +412,16 @@
             to_up(t).wait_recv()
 
     def far_pass(j):
-        arrival(2 * j).wait_recv()
-
-        @pl.when(jnp.logical_and(has_up, jnp.logical_not(edge_up)))
-        def _():
-            relay_up(j).start()
-
-        arrival(2 * j + 1).wait_recv()
-
-        @pl.when(jnp.logical_and(has_down, jnp.logical_not(edge_down)))
-        def _():
-            relay_down(j).start()
+        for leads, h, there, copy in ((odd, 0, has_up, relay_up), (jnp.logical_not(odd), 1, has_down, relay_down)):
+            @pl.when(leads)
+            def _():
+                arrival(2 * j + h).wait_recv()
+
+                @pl.when(there)
+                def _():
+                    copy(j).start()
+
+                arrival(2 * j + 1 - h).wait_recv()
 
     def near_pass(j):
         to_prev(j).wait_recv()

time: 23.9 us -> 23.9 us (level)
  no operation moved by 1% of the time
where the time goes in v9:
time: 23.9 us; the launch traced here: 23.8 us
  Pallas kernels  22.3 us (93%)
  local copies, waits for them, and re-layouts  1.49 us (6%)
    pallas_call x1, Pallas kernels, on_device(): pl.pallas_call(functools.partial(kernel, secs_axis, rows_axis), out_shape...  22.3 us
    unnamed x1, local copies, waits for them, and re-layouts  1.49 us

profile of v9, /device:TPU:127, one launch (start us, length us, event | category | flops | bytes accessed | tf_op | source)
XLA Modules:
  0.0 23.8 jit_solution(3508618408084351140)
XLA Ops:
  0.0 22.3 %shard_map.100 = f32[4,2,5,128,128]{4,3,2,1,0:T(8,128)S(1)} custom-call(s32[4,1,2,5]{3,2,1,0:T(2,128)} %bitcast.4, s32[2,4]{1,0:T(2,128)} %bitcast.5, s32[4,1,5]{2,1,0:T(1,128)} %tissue_hbm.1, bf16[4,128,640]{2,1,0:T(8,128)(2,1)} %img.1, bf16[256,256]{1,0:T(8,128)(2,1)} %constant.12.clone.refs_0_, bf16[2,256,256]{2,1,0:T(8,128)(2,1)} %constant.13.clone.refs_1_, ...), custom_call_target="tpu_custom_call" | custom-call | flops 6000000000 | bytes 8000000 | tf_op jit(solution)/shard_map/pallas_call | solution.py:544
  22.3 1.5 %copy.17 = f32[4,2,1,5,16384]{4,2,3,1,0:T(1,128)} copy(f32[4,2,1,5,16384]{4,2,3,1,0:T(1,128)S(1)} %bitcast.3) | data formatting | bytes 5242880
